TPU v7x, 256 devices: a whole 4x4x8 slice. The times are simulated.
256 devices in a mesh: section: 16 (over y_lo, z), expert: 16 (over x, y_hi, core).
Axes of the slice: x: 4, y: 4 (y_hi: 2, y_lo: 2; y = y_hi * 2 + y_lo), z: 8, core: 2. Of those that a mesh axis runs over, the one named last changes fastest.
Arguments:
- carried: bfloat16 [16, 2048, 2048], P('section', 'expert'), may hold values from -6 to 6
- saved_rows: bfloat16 [16, 2048, 2048], P('section', 'expert'), may hold values from -6 to 6
- returned: bfloat16 [16, 2048, 2048], P('section', 'expert'), may hold values from -6 to 6
- fwd_ids: int32 [16, 2048, 2], P('section', 'expert'), may hold values from 0 to 3, all different within a row; in each aligned block of 128 rows (0 to 127, 128 to 255, ..., all dimensions but the last counted through in order) at most 72 rows name the same one
- fwd_gates: float32 [16, 2048, 2], P('section', 'expert'), may hold values from 0.2 to 1
- bwd_ids: int32 [16, 2048, 2], P('section', 'expert'), may hold values from 0 to 3, all different within a row; in each aligned block of 128 rows (0 to 127, 128 to 255, ..., all dimensions but the last counted through in order) at most 72 rows name the same one
- bwd_gates: float32 [16, 2048, 2], P('section', 'expert'), may hold values from 0.2 to 1
- gate_w: bfloat16 [16, 2048, 4096], P('section', None, 'expert'), may hold values from -0.125 to 0.125
- up_w: bfloat16 [16, 2048, 4096], P('section', None, 'expert'), may hold values from -0.125 to 0.125
- down_w: bfloat16 [16, 4096, 2048], P('section', 'expert'), may hold values from -0.1875 to 0.1875
Outputs:
- next_input: bfloat16 [16, 2048, 2048], P('section', 'expert')
- grad_input: bfloat16 [16, 2048, 2048], P('section', 'expert')
- gate_grad: float32 [16, 2048, 4096], P('section', None, 'expert')
- up_grad: float32 [16, 2048, 4096], P('section', None, 'expert')
- down_grad: float32 [16, 4096, 2048], P('section', 'expert')
Inputs may be any that keep to these rules, and one draw needn't show every extreme that they name: `fwd_ids`: the 2 ids of a token differ. In each aligned block of 128 tokens (one device's tokens of one section) each expert is named by at most 72 tokens, a bound that some block reaches. `bwd_ids`: the 2 ids of a token differ. In each aligned block of 128 tokens each expert is named by at most 72 tokens, a bound that some block reaches.
All inputs are finite; a program needn't handle non-finite values.
Results may differ from a plain program's by a relative error of at most 0.0052.
Values may be sent and summed in bfloat16 or wider, within the bound.
A program may use at most 128 MiB of HBM per device.

v0:
```python
import jax
import jax.numpy as jnp
from jax import lax
from jax.sharding import PartitionSpec as P

E_WIN = 4
CAP = 72


def passed_along(value, axis, steps):
    count = lax.axis_size(axis)
    pairs = [(source, (source + steps) % count) for source in range(count)]
    return lax.ppermute(value, axis, pairs)


def slot_table(route_ids):
    flat = route_ids.reshape(-1)
    onehot = (flat[:, None] == jnp.arange(E_WIN, dtype=jnp.int32)[None, :]).astype(jnp.int32)
    before = jnp.cumsum(onehot, axis=0) - onehot
    ranking = jnp.sum(before * onehot, axis=1)
    return (flat * CAP + ranking).reshape(route_ids.shape)


def spread(slots, weights):
    columns = jnp.arange(E_WIN * CAP, dtype=jnp.int32)
    match = (slots[:, :, None] == columns[None, None, :]).astype(jnp.float32)
    return jnp.sum(weights[:, :, None] * match, axis=1)


def pick_rows(table, token_rows):
    return jnp.einsum(
        "tc,td->cd", table.astype(jnp.bfloat16), token_rows, preferred_element_type=jnp.float32
    ).astype(jnp.bfloat16)


def fan_out(buffer, group_size):
    return jnp.repeat(buffer.reshape(E_WIN, CAP, buffer.shape[-1]), group_size, axis=0)


def partial_total(returned_parts, group_size):
    width = returned_parts.shape[-1]
    summed = returned_parts.reshape(E_WIN, group_size, CAP, width).astype(jnp.float32).sum(axis=1)
    return summed.reshape(E_WIN * CAP, width)


def token_sum(totals, slots, weights):
    picked = jnp.take(totals, slots.reshape(-1), axis=0).reshape(
        slots.shape[0], slots.shape[1], totals.shape[-1]
    )
    return jnp.sum(weights[:, :, None] * picked, axis=1)


def body(
    carried, saved_rows, returned, fwd_ids, fwd_gates, bwd_ids, bwd_gates, gate_w, up_w, down_w
):
    devices = lax.axis_size("expert")
    group_size = devices // E_WIN
    layer_in = passed_along(carried, "section", 1)[0]
    cotangent = passed_along(returned, "section", -1)[0]
    saved_in = saved_rows[0]
    fwd_route = fwd_ids[0]
    bwd_route = bwd_ids[0]
    fwd_weight = fwd_gates[0]
    bwd_weight = bwd_gates[0]
    gate_part = gate_w[0]
    up_part = up_w[0]
    down_part = down_w[0]
    width = layer_in.shape[1]
    fwd_slots = slot_table(fwd_route)
    bwd_slots = slot_table(bwd_route)
    fwd_ones = spread(fwd_slots, jnp.ones(fwd_weight.shape, jnp.float32))
    bwd_ones = spread(bwd_slots, jnp.ones(bwd_weight.shape, jnp.float32))
    slot_gates = jnp.sum(spread(bwd_slots, bwd_weight), axis=0)
    send_rows = fan_out(pick_rows(fwd_ones, layer_in), group_size)
    recv_rows = lax.all_to_all(send_rows, "expert", split_axis=0, concat_axis=0, tiled=True)
    send_saved = fan_out(pick_rows(bwd_ones, saved_in), group_size)
    chosen_grads = pick_rows(bwd_ones, cotangent)
    gated = (slot_gates[:, None] * chosen_grads.astype(jnp.float32)).astype(jnp.bfloat16)
    send_scaled = fan_out(gated, group_size)
    recv_saved, recv_scaled = (
        lax.all_to_all(send_saved, "expert", split_axis=0, concat_axis=0, tiled=True),
        lax.all_to_all(send_scaled, "expert", split_axis=0, concat_axis=0, tiled=True),
    )
    token_rows = recv_rows.reshape(-1, width)
    pre_gate = jnp.dot(token_rows, gate_part, preferred_element_type=jnp.float32)
    pre_up = jnp.dot(token_rows, up_part, preferred_element_type=jnp.float32)
    hidden = (pre_gate * jax.nn.sigmoid(pre_gate) * pre_up).astype(jnp.bfloat16)
    fwd_parts = (
        jnp.dot(hidden, down_part, preferred_element_type=jnp.float32)
        .astype(jnp.bfloat16)
        .reshape(devices, CAP, width)
    )
    saved_flat = recv_saved.reshape(-1, width)
    scaled_flat = recv_scaled.reshape(-1, width)
    pre_gate2 = jnp.dot(saved_flat, gate_part, preferred_element_type=jnp.float32)
    pre_up2 = jnp.dot(saved_flat, up_part, preferred_element_type=jnp.float32)
    sigma2 = jax.nn.sigmoid(pre_gate2)
    swish = pre_gate2 * sigma2
    hidden2 = (swish * pre_up2).astype(jnp.bfloat16)
    grad_hidden = jnp.einsum(
        "rd,hd->rh", scaled_flat, down_part, preferred_element_type=jnp.float32
    )
    grad_gate_pre = (grad_hidden * pre_up2 * sigma2 * (1.0 + pre_gate2 * (1.0 - sigma2))).astype(
        jnp.bfloat16
    )
    grad_up_pre = (grad_hidden * swish).astype(jnp.bfloat16)
    back_parts = jnp.einsum(
        "rh,dh->rd", grad_gate_pre, gate_part, preferred_element_type=jnp.float32
    )
    back_parts = back_parts + jnp.einsum(
        "rh,dh->rd", grad_up_pre, up_part, preferred_element_type=jnp.float32
    )
    back_parts = back_parts.astype(jnp.bfloat16).reshape(devices, CAP, width)
    gate_grad = jnp.einsum(
        "rd,rh->dh", saved_flat, grad_gate_pre, preferred_element_type=jnp.float32
    )
    up_grad = jnp.einsum("rd,rh->dh", saved_flat, grad_up_pre, preferred_element_type=jnp.float32)
    down_grad = jnp.einsum("rh,rd->hd", hidden2, scaled_flat, preferred_element_type=jnp.float32)
    fwd_back = lax.all_to_all(fwd_parts, "expert", split_axis=0, concat_axis=0, tiled=True)
    bwd_back = lax.all_to_all(back_parts, "expert", split_axis=0, concat_axis=0, tiled=True)
    output_sum = layer_in.astype(jnp.float32) + token_sum(
        partial_total(fwd_back, group_size), fwd_slots, fwd_weight
    )
    input_grad = cotangent.astype(jnp.float32) + token_sum(
        partial_total(bwd_back, group_size), bwd_slots, jnp.ones(bwd_weight.shape, jnp.float32)
    )
    return (
        output_sum.astype(jnp.bfloat16)[None],
        input_grad.astype(jnp.bfloat16)[None],
        gate_grad[None],
        up_grad[None],
        down_grad[None],
    )


def solution(mesh):
    placed = (
        P("section", "expert", None),
        P("section", "expert", None),
        P("section", "expert", None),
        P("section", "expert", None),
        P("section", "expert", None),
        P("section", "expert", None),
        P("section", "expert", None),
        P("section", None, "expert"),
        P("section", None, "expert"),
        P("section", "expert", None),
    )
    return jax.shard_map(
        body,
        mesh=mesh,
        in_specs=placed,
        out_specs=(
            P("section", "expert", None),
            P("section", "expert", None),
            P("section", None, "expert"),
            P("section", None, "expert"),
            P("section", "expert", None),
        ),
        check_vma=False,
    )
```

profile of v0, /device:TPU:245, one launch (start us, length us, event | category | flops | bytes accessed | tf_op | source)
XLA Modules:
  0.0 421.2 jit_solution(3286757524957807532)
XLA Ops:
  8.8 7.7 %all-to-all-start.3 = ((bf16[16,72,2048]{2,1,0:T(8,128)(2,1)}), bf16[16,72,2048]{2,1,0:T(8,128)(2,1)}, u32[]{:S(2)}, u32[]{:S(2)}) async-start(bf16[16,72,2048]{2,1,0:T(8,128)(2,1)} %bitcast.125), calls=%async_computation.3 | async-start | bytes 9437184 | tf_op jit(solution)/shard_map/all_to_all | solution.py:81
  18.9 19.9 %collective-permute-done = bf16[1,128,2048]{2,1,0:T(8,128)(2,1)S(1)} collective-permute-done((bf16[1,128,2048]{2,1,0:T(8,128)(2,1)S(1)}, bf16[1,128,2048]{2,1,0:T(8,128)(2,1)S(1)}, u32[]{:S(2)}, u32[]{:S(2)}) %collective-permute-start) | collective-permute-done | bytes 524320 | tf_op jit(solution)/shard_map/ppermute | solution.py:13
  39.3 44.7 %all-to-all-done.3 = bf16[16,72,2048]{2,1,0:T(8,128)(2,1)} async-done(((bf16[16,72,2048]{2,1,0:T(8,128)(2,1)}), bf16[16,72,2048]{2,1,0:T(8,128)(2,1)}, u32[]{:S(2)}, u32[]{:S(2)}) %all-to-all-start.3) | async-done | bytes 4718624 | tf_op jit(solution)/shard_map/all_to_all | solution.py:81
  86.7 7.2 %all-to-all-start = ((bf16[16,72,2048]{2,1,0:T(8,128)(2,1)}), bf16[16,72,2048]{2,1,0:T(8,128)(2,1)}, u32[]{:S(2)}, u32[]{:S(2)}) async-start(bf16[16,72,2048]{2,1,0:T(8,128)(2,1)} %bitcast.126), calls=%async_computation | async-start | bytes 9437184 | tf_op jit(solution)/shard_map/all_to_all | solution.py:75
  94.8 25.4 %collective-permute-done.1 = bf16[1,128,2048]{2,1,0:T(8,128)(2,1)S(1)} collective-permute-done((bf16[1,128,2048]{2,1,0:T(8,128)(2,1)S(1)}, bf16[1,128,2048]{2,1,0:T(8,128)(2,1)S(1)}, u32[]{:S(2)}, u32[]{:S(2)}) %collective-permute-start.1) | collective-permute-done | bytes 524320 | tf_op jit(solution)/shard_map/ppermute | solution.py:13
  121.5 48.5 %all-to-all-done = bf16[16,72,2048]{2,1,0:T(8,128)(2,1)} async-done(((bf16[16,72,2048]{2,1,0:T(8,128)(2,1)}), bf16[16,72,2048]{2,1,0:T(8,128)(2,1)}, u32[]{:S(2)}, u32[]{:S(2)}) %all-to-all-start) | async-done | bytes 4718624 | tf_op jit(solution)/shard_map/all_to_all | solution.py:75
  172.8 7.4 %all-to-all-start.2 = ((bf16[16,72,2048]{2,1,0:T(8,128)(2,1)}), bf16[16,72,2048]{2,1,0:T(8,128)(2,1)}, u32[]{:S(2)}, u32[]{:S(2)}) async-start(bf16[16,72,2048]{2,1,0:T(8,128)(2,1)} %bitcast.127), calls=%async_computation.2 | async-start | bytes 9437184 | tf_op jit(solution)/shard_map/all_to_all | solution.py:82
  180.1 4.7 %fusion.25 = f32[1152,256]{1,0:T(8,128)} fusion(bf16[1152,2048]{1,0:T(8,128)(2,1)} %bitcast.7, bf16[1,2048,256]{2,1,0:T(8,128)(2,1)S(1)} %copy-done.7), kind=kOutput, calls=%fused_computation.44 | convolution fusion | flops 1207959552 | bytes 6946816 | tf_op jit(solution)/shard_map/dot_general | solution.py:85
  184.9 10.0 %convolution_convert_fusion = bf16[1152,2048]{1,0:T(8,128)(2,1)} fusion(bf16[1152,2048]{1,0:T(8,128)(2,1)} %bitcast.7, f32[1152,256]{1,0:T(8,128)} %fusion.25, bf16[1,256,2048]{2,1,0:T(8,128)(2,1)} %param.21, bf16[1,2048,256]{2,1,0:T(8,128)(2,1)S(1)} %copy-done), kind=kOutput, calls=%fused_computation.6 | convolution fusion | flops 2420047872 | bytes 12713984 | tf_op jit(solution)/shard_map/dot_general | solution.py:89
  194.9 52.8 %all-to-all-done.2 = bf16[16,72,2048]{2,1,0:T(8,128)(2,1)} async-done(((bf16[16,72,2048]{2,1,0:T(8,128)(2,1)}), bf16[16,72,2048]{2,1,0:T(8,128)(2,1)}, u32[]{:S(2)}, u32[]{:S(2)}) %all-to-all-start.2) | async-done | bytes 4718624 | tf_op jit(solution)/shard_map/all_to_all | solution.py:82
  247.6 7.1 %all-to-all-start.1 = ((bf16[16,72,2048]{2,1,0:T(8,128)(2,1)}), bf16[16,72,2048]{2,1,0:T(8,128)(2,1)}, u32[]{:S(2)}, u32[]{:S(2)}) async-start(bf16[16,72,2048]{2,1,0:T(8,128)(2,1)} %bitcast.129), calls=%async_computation.1 | async-start | bytes 9437184 | tf_op jit(solution)/shard_map/all_to_all | solution.py:119
  254.7 3.7 fusion.23
  258.5 4.2 fusion.17
  262.7 4.5 %multiply_convert_fusion.1 = (bf16[1152,256]{1,0:T(8,128)(2,1)S(1)}, bf16[1152,256]{1,0:T(8,128)(2,1)S(1)}) fusion(f32[1152,256]{1,0:T(8,128)S(1)} %fusion.23, f32[1152,256]{1,0:T(8,128)S(1)} %fusion.17, bf16[1152,2048]{1,0:T(8,128)(2,1)} %bitcast.22, bf16[1,256,2048]{2,1,0:T(8,128)(2,1)S(1)} %copy-done.10), kind=kOutput, calls=%fused_computation.20 | convolution fusion | flops 1211793408 | bytes 9306112 | tf_op jit(solution)/shard_map/rd,hd->rh/dot_general | solution.py:100
  268.7 3.7 fusion
  272.4 49.8 %all-to-all-done.1 = bf16[16,72,2048]{2,1,0:T(8,128)(2,1)} async-done(((bf16[16,72,2048]{2,1,0:T(8,128)(2,1)}), bf16[16,72,2048]{2,1,0:T(8,128)(2,1)}, u32[]{:S(2)}, u32[]{:S(2)}) %all-to-all-start.1) | async-done | bytes 4718624 | tf_op jit(solution)/shard_map/all_to_all | solution.py:119
  322.2 7.2 %all-to-all-start.4 = ((bf16[16,72,2048]{2,1,0:T(8,128)(2,1)}), bf16[16,72,2048]{2,1,0:T(8,128)(2,1)}, u32[]{:S(2)}, u32[]{:S(2)}) async-start(bf16[16,72,2048]{2,1,0:T(8,128)(2,1)} %bitcast.128), calls=%async_computation.4 | async-start | bytes 9437184 | tf_op jit(solution)/shard_map/all_to_all | solution.py:120
  329.6 5.2 %convolution_bitcast_fusion.1 = f32[1,2048,256]{2,1,0:T(8,128)} fusion(bf16[1152,2048]{1,0:T(8,128)(2,1)} %bitcast.26, bf16[1152,256]{1,0:T(8,128)(2,1)S(1)} %get-tuple-element.12), kind=kOutput, calls=%fused_computation.9 | convolution fusion | flops 1207959552 | bytes 7405568 | tf_op jit(solution)/shard_map/rd,rh->dh/dot_general | solution.py:117
  334.8 5.4 %convolution_bitcast_fusion.2 = f32[1,2048,256]{2,1,0:T(8,128)} fusion(bf16[1152,2048]{1,0:T(8,128)(2,1)} %bitcast.26, bf16[1152,256]{1,0:T(8,128)(2,1)S(1)} %get-tuple-element.13), kind=kOutput, calls=%fused_computation.10 | convolution fusion | flops 1207959552 | bytes 7405568 | tf_op jit(solution)/shard_map/rd,rh->dh/dot_general | solution.py:114
  340.2 5.3 %convolution_bitcast_fusion = f32[1,256,2048]{2,1,0:T(8,128)} fusion(bf16[1152,2048]{1,0:T(8,128)(2,1)} %bitcast.22, f32[1152,256]{1,0:T(8,128)S(1)} %copy-done.16, f32[1152,256]{1,0:T(8,128)S(1)} %copy-done.14), kind=kOutput, calls=%fused_computation.8 | convolution fusion | flops 1209729024 | bytes 9175040 | tf_op jit(solution)/shard_map/rh,rd->hd/dot_general | solution.py:118
  355.8 41.1 %all-to-all-done.4 = bf16[16,72,2048]{2,1,0:T(8,128)(2,1)} async-done(((bf16[16,72,2048]{2,1,0:T(8,128)(2,1)}), bf16[16,72,2048]{2,1,0:T(8,128)(2,1)}, u32[]{:S(2)}, u32[]{:S(2)}) %all-to-all-start.4) | async-done | bytes 4718624 | tf_op jit(solution)/shard_map/all_to_all | solution.py:120
  406.3 3.6 reshape.145
  409.9 4.1 multiply_reduce_fusion
  414.0 4.3 %reduce_sum.104 = f32[128,2048]{1,0:T(8,128)S(1)} reduce(f32[128,2,2048]{2,1,0:T(2,128)} %reshape.145, f32[]{:T(128)} %constant.23.clone.1), dimensions={1}, to_apply=%region_12.14 | reduce | flops 262144 | bytes 3145732 | tf_op jit(solution)/shard_map/reduce_sum | solution.py:50
  (89 shorter events, 42.8 us)
Async XLA Ops:
  0.6 184.3 %copy-start = (bf16[1,2048,256]{2,1,0:T(8,128)(2,1)S(1)}, bf16[1,2048,256]{2,1,0:T(8,128)(2,1)}, u32[]{:S(2)}) copy-start(bf16[1,2048,256]{2,1,0:T(8,128)(2,1)} %param.20) | copy-start | bytes 3145732
  8.8 7.7 %copy-start.11 = (bf16[1,128,2048]{2,1,0:T(8,128)(2,1)S(1)}, bf16[1,128,2048]{2,1,0:T(8,128)(2,1)}, u32[]{:S(2)}) copy-start(bf16[1,128,2048]{2,1,0:T(8,128)(2,1)} %param.12) | copy-start | bytes 1572868
  8.8 7.8 %copy-start.8 = (s32[1,128,2]{1,2,0:T(2,128)S(1)}, s32[1,128,2]{1,2,0:T(2,128)}, u32[]{:S(2)}) copy-start(s32[1,128,2]{1,2,0:T(2,128)} %param.15) | copy-start | bytes 3076
  8.8 75.2 %all-to-all-start.3 = ((bf16[16,72,2048]{2,1,0:T(8,128)(2,1)}), bf16[16,72,2048]{2,1,0:T(8,128)(2,1)}, u32[]{:S(2)}, u32[]{:S(2)}) async-start(bf16[16,72,2048]{2,1,0:T(8,128)(2,1)} %bitcast.125), calls=%async_computation.3 | async-start | bytes 9437184 | tf_op jit(solution)/shard_map/all_to_all | solution.py:81
  16.5 22.3 %collective-permute-start = (bf16[1,128,2048]{2,1,0:T(8,128)(2,1)S(1)}, bf16[1,128,2048]{2,1,0:T(8,128)(2,1)S(1)}, u32[]{:S(2)}, u32[]{:S(2)}) collective-permute-start(bf16[1,128,2048]{2,1,0:T(8,128)(2,1)S(1)} %copy-done.11), channel_id=1, source_target_pairs={{0,16},{16,32},{32,48},{48,64},{64,80},{80,96},{96,112},{112,128},... | collective-permute-start | bytes 1572872 | tf_op jit(solution)/shard_map/ppermute | solution.py:13
  38.8 47.9 %copy-start.4 = (bf16[1,128,2048]{2,1,0:T(8,128)(2,1)}, bf16[1,128,2048]{2,1,0:T(8,128)(2,1)S(1)}, u32[]{:S(2)}) copy-start(bf16[1,128,2048]{2,1,0:T(8,128)(2,1)S(1)} %collective-permute-done) | copy-start | bytes 1572868
  86.7 7.2 %copy-start.12 = (bf16[1,128,2048]{2,1,0:T(8,128)(2,1)S(1)}, bf16[1,128,2048]{2,1,0:T(8,128)(2,1)}, u32[]{:S(2)}) copy-start(bf16[1,128,2048]{2,1,0:T(8,128)(2,1)} %param.14) | copy-start | bytes 1572868
  86.7 83.3 %all-to-all-start = ((bf16[16,72,2048]{2,1,0:T(8,128)(2,1)}), bf16[16,72,2048]{2,1,0:T(8,128)(2,1)}, u32[]{:S(2)}, u32[]{:S(2)}) async-start(bf16[16,72,2048]{2,1,0:T(8,128)(2,1)} %bitcast.126), calls=%async_computation | async-start | bytes 9437184 | tf_op jit(solution)/shard_map/all_to_all | solution.py:75
  94.0 26.2 %collective-permute-start.1 = (bf16[1,128,2048]{2,1,0:T(8,128)(2,1)S(1)}, bf16[1,128,2048]{2,1,0:T(8,128)(2,1)S(1)}, u32[]{:S(2)}, u32[]{:S(2)}) collective-permute-start(bf16[1,128,2048]{2,1,0:T(8,128)(2,1)S(1)} %copy-done.12), channel_id=1, source_target_pairs={{0,240},{16,0},{32,16},{48,32},{64,48},{80,64},{96,80},{112,96},{1... | collective-permute-start | bytes 1572872 | tf_op jit(solution)/shard_map/ppermute | solution.py:13
  120.2 0.8 copy-start.5
  172.7 7.4 %copy-start.7 = (bf16[1,2048,256]{2,1,0:T(8,128)(2,1)S(1)}, bf16[1,2048,256]{2,1,0:T(8,128)(2,1)}, u32[]{:S(2)}) copy-start(bf16[1,2048,256]{2,1,0:T(8,128)(2,1)} %param.19) | copy-start | bytes 3145732
  172.8 74.9 %all-to-all-start.2 = ((bf16[16,72,2048]{2,1,0:T(8,128)(2,1)}), bf16[16,72,2048]{2,1,0:T(8,128)(2,1)}, u32[]{:S(2)}, u32[]{:S(2)}) async-start(bf16[16,72,2048]{2,1,0:T(8,128)(2,1)} %bitcast.127), calls=%async_computation.2 | async-start | bytes 9437184 | tf_op jit(solution)/shard_map/all_to_all | solution.py:82
  247.6 74.6 %all-to-all-start.1 = ((bf16[16,72,2048]{2,1,0:T(8,128)(2,1)}), bf16[16,72,2048]{2,1,0:T(8,128)(2,1)}, u32[]{:S(2)}, u32[]{:S(2)}) async-start(bf16[16,72,2048]{2,1,0:T(8,128)(2,1)} %bitcast.129), calls=%async_computation.1 | async-start | bytes 9437184 | tf_op jit(solution)/shard_map/all_to_all | solution.py:119
  258.5 4.2 %copy-start.13 = (f32[1152,256]{1,0:T(8,128)}, f32[1152,256]{1,0:T(8,128)S(1)}, u32[]{:S(2)}) copy-start(f32[1152,256]{1,0:T(8,128)S(1)} %fusion.23) | copy-start | bytes 3538948
  258.5 4.2 %copy-start.10 = (bf16[1,256,2048]{2,1,0:T(8,128)(2,1)S(1)}, bf16[1,256,2048]{2,1,0:T(8,128)(2,1)}, u32[]{:S(2)}) copy-start(bf16[1,256,2048]{2,1,0:T(8,128)(2,1)} %param.21) | copy-start | bytes 3145732
  262.7 4.6 %copy-start.15 = (f32[1152,256]{1,0:T(8,128)}, f32[1152,256]{1,0:T(8,128)S(1)}, u32[]{:S(2)}) copy-start(f32[1152,256]{1,0:T(8,128)S(1)} %fusion.17) | copy-start | bytes 3538948
  322.2 7.2 %copy-start.9 = (f32[1,128,2]{1,2,0:T(2,128)S(1)}, f32[1,128,2]{1,2,0:T(2,128)}, u32[]{:S(2)}) copy-start(f32[1,128,2]{1,2,0:T(2,128)} %param.16) | copy-start | bytes 3076
  322.2 74.7 %all-to-all-start.4 = ((bf16[16,72,2048]{2,1,0:T(8,128)(2,1)}), bf16[16,72,2048]{2,1,0:T(8,128)(2,1)}, u32[]{:S(2)}, u32[]{:S(2)}) async-start(bf16[16,72,2048]{2,1,0:T(8,128)(2,1)} %bitcast.128), calls=%async_computation.4 | async-start | bytes 9437184 | tf_op jit(solution)/shard_map/all_to_all | solution.py:120
  334.8 5.4 %copy-start.14 = (f32[1152,256]{1,0:T(8,128)S(1)}, f32[1152,256]{1,0:T(8,128)}, u32[]{:S(2)}) copy-start(f32[1152,256]{1,0:T(8,128)} %copy-done.13) | copy-start | bytes 3538948
  334.8 5.4 %copy-start.16 = (f32[1152,256]{1,0:T(8,128)S(1)}, f32[1152,256]{1,0:T(8,128)}, u32[]{:S(2)}) copy-start(f32[1152,256]{1,0:T(8,128)} %copy-done.15) | copy-start | bytes 3538948
  406.3 3.6 copy-start.2
  414.0 4.3 %copy-start.3 = (f32[128,2048]{1,0:T(8,128)S(1)}, f32[128,2048]{1,0:T(8,128)}, u32[]{:S(2)}) copy-start(f32[128,2048]{1,0:T(8,128)} %multiply_reduce_fusion) | copy-start | bytes 3145732
  414.0 7.2 %copy-start.1 = (bf16[1,2048,256]{2,1,0:T(8,128)(2,1)S(1)}, bf16[1,2048,256]{2,1,0:T(8,128)(2,1)}, u32[]{:S(2)}) copy-start(bf16[1,2048,256]{2,1,0:T(8,128)(2,1)} %param.20) | copy-start | bytes 3145732
  418.2 2.0 copy-start.6
where the time goes:
time: 422 us; the launch traced here: 421 us
  waiting for transfers between devices  282 us (67%)
  matrix products  50.6 us (12%)
  starting transfers between devices  37.4 us (9%)
  other arithmetic  26.9 us (6%)
  local copies, waits for them, and re-layouts  23.1 us (5%)
    all_to_all x1, waiting for transfers between devices, body(): lax.all_to_all(send_scaled, 'expert', split_axis=0, concat_axis=0, tiled=...  52.8 us
    all_to_all x1, waiting for transfers between devices, body(): lax.all_to_all(fwd_parts, 'expert', split_axis=0, concat_axis=0, tiled=True)  49.8 us
    all_to_all x1, waiting for transfers between devices, body(): lax.all_to_all(send_rows, 'expert', split_axis=0, concat_axis=0, tiled=True)  48.5 us
    ppermute x2, waiting for transfers between devices, passed_along(): return lax.ppermute(value, axis, pairs)  45.3 us
    all_to_all x1, waiting for transfers between devices, body(): lax.all_to_all(send_saved, 'expert', split_axis=0, concat_axis=0, tiled=T...  44.7 us
    all_to_all x1, waiting for transfers between devices, body(): lax.all_to_all(back_parts, 'expert', split_axis=0, concat_axis=0, tiled=T...  41.1 us
    dot_general x1, matrix products, body(): jnp.dot(hidden, down_part, preferred_element_type=jnp.float32)  9.96 us
  transfers between devices with their start and end apart: 7, of which 7 were waited for; matrix products, arithmetic and copies ran while one was open for 15% of the time, Pallas kernels for 0%

commit v1 on v0

--- a/solution.py
+++ b/solution.py
@@ -16,7 +16,9 @@
 def slot_table(route_ids):
     flat = route_ids.reshape(-1)
     onehot = (flat[:, None] == jnp.arange(E_WIN, dtype=jnp.int32)[None, :]).astype(jnp.int32)
-    before = jnp.cumsum(onehot, axis=0) - onehot
+    rows = flat.shape[0]
+    earlier = (jnp.arange(rows)[:, None] > jnp.arange(rows)[None, :]).astype(jnp.bfloat16)
+    before = jnp.dot(earlier, onehot.astype(jnp.bfloat16), preferred_element_type=jnp.float32).astype(jnp.int32)
     ranking = jnp.sum(before * onehot, axis=1)
     return (flat * CAP + ranking).reshape(route_ids.shape)
 

time: 422 us -> 420 us (level)
  transfers between devices with their start and end apart: 7 -> 7, of which waited for: 7 -> 7; matrix products, arithmetic and copies ran while one was open for 15% -> 14% of each run, Pallas kernels for 0% -> 0%
where the time goes in v1:
time: 420 us
  waiting for transfers between devices  284 us (68%)
  matrix products  51 us (12%)
  starting transfers between devices  37.4 us (9%)
  other arithmetic  24.1 us (6%)
  local copies, waits for them, and re-layouts  22.2 us (5%)
    all_to_all x1, waiting for transfers between devices, body(): lax.all_to_all(send_scaled, 'expert', split_axis=0, concat_axis=0, tiled=...  52.8 us
    all_to_all x1, waiting for transfers between devices, body(): lax.all_to_all(fwd_parts, 'expert', split_axis=0, concat_axis=0, tiled=True)  49.8 us
    all_to_all x1, waiting for transfers between devices, body(): lax.all_to_all(send_rows, 'expert', split_axis=0, concat_axis=0, tiled=True)  48.6 us
    ppermute x2, waiting for transfers between devices, passed_along(): return lax.ppermute(value, axis, pairs)  46.8 us
    all_to_all x1, waiting for transfers between devices, body(): lax.all_to_all(send_saved, 'expert', split_axis=0, concat_axis=0, tiled=T...  44.7 us
    all_to_all x1, waiting for transfers between devices, body(): lax.all_to_all(back_parts, 'expert', split_axis=0, concat_axis=0, tiled=T...  41.1 us
    dot_general x1, matrix products, body(): jnp.dot(hidden, down_part, preferred_element_type=jnp.float32)  9.96 us
  transfers between devices with their start and end apart: 7, of which 7 were waited for; matrix products, arithmetic and copies ran while one was open for 14% of the time, Pallas kernels for 0%

profile of v1, /device:TPU:245, one launch (start us, length us, event | category | flops | bytes accessed | tf_op | source)
XLA Modules:
  0.0 419.5 jit_solution(16676901397040972306)
XLA Ops:
  7.2 7.7 %all-to-all-start.3 = ((bf16[16,72,2048]{2,1,0:T(8,128)(2,1)}), bf16[16,72,2048]{2,1,0:T(8,128)(2,1)}, u32[]{:S(2)}, u32[]{:S(2)}) async-start(bf16[16,72,2048]{2,1,0:T(8,128)(2,1)} %bitcast.87), calls=%async_computation.3 | async-start | bytes 9437184 | tf_op jit(solution)/shard_map/all_to_all | solution.py:83
  15.8 21.5 %collective-permute-done = bf16[1,128,2048]{2,1,0:T(8,128)(2,1)S(1)} collective-permute-done((bf16[1,128,2048]{2,1,0:T(8,128)(2,1)S(1)}, bf16[1,128,2048]{2,1,0:T(8,128)(2,1)S(1)}, u32[]{:S(2)}, u32[]{:S(2)}) %collective-permute-start) | collective-permute-done | bytes 524320 | tf_op jit(solution)/shard_map/ppermute | solution.py:13
  37.7 44.7 %all-to-all-done.3 = bf16[16,72,2048]{2,1,0:T(8,128)(2,1)} async-done(((bf16[16,72,2048]{2,1,0:T(8,128)(2,1)}), bf16[16,72,2048]{2,1,0:T(8,128)(2,1)}, u32[]{:S(2)}, u32[]{:S(2)}) %all-to-all-start.3) | async-done | bytes 4718624 | tf_op jit(solution)/shard_map/all_to_all | solution.py:83
  85.2 7.2 %all-to-all-start = ((bf16[16,72,2048]{2,1,0:T(8,128)(2,1)}), bf16[16,72,2048]{2,1,0:T(8,128)(2,1)}, u32[]{:S(2)}, u32[]{:S(2)}) async-start(bf16[16,72,2048]{2,1,0:T(8,128)(2,1)} %bitcast.88), calls=%async_computation | async-start | bytes 9437184 | tf_op jit(solution)/shard_map/all_to_all | solution.py:77
  93.2 25.3 %collective-permute-done.1 = bf16[1,128,2048]{2,1,0:T(8,128)(2,1)S(1)} collective-permute-done((bf16[1,128,2048]{2,1,0:T(8,128)(2,1)S(1)}, bf16[1,128,2048]{2,1,0:T(8,128)(2,1)S(1)}, u32[]{:S(2)}, u32[]{:S(2)}) %collective-permute-start.1) | collective-permute-done | bytes 524320 | tf_op jit(solution)/shard_map/ppermute | solution.py:13
  119.8 48.6 %all-to-all-done = bf16[16,72,2048]{2,1,0:T(8,128)(2,1)} async-done(((bf16[16,72,2048]{2,1,0:T(8,128)(2,1)}), bf16[16,72,2048]{2,1,0:T(8,128)(2,1)}, u32[]{:S(2)}, u32[]{:S(2)}) %all-to-all-start) | async-done | bytes 4718624 | tf_op jit(solution)/shard_map/all_to_all | solution.py:77
  171.2 7.4 %all-to-all-start.2 = ((bf16[16,72,2048]{2,1,0:T(8,128)(2,1)}), bf16[16,72,2048]{2,1,0:T(8,128)(2,1)}, u32[]{:S(2)}, u32[]{:S(2)}) async-start(bf16[16,72,2048]{2,1,0:T(8,128)(2,1)} %bitcast.89), calls=%async_computation.2 | async-start | bytes 9437184 | tf_op jit(solution)/shard_map/all_to_all | solution.py:84
  178.6 4.7 %fusion.29 = f32[1152,256]{1,0:T(8,128)} fusion(bf16[1152,2048]{1,0:T(8,128)(2,1)} %bitcast.5, bf16[1,2048,256]{2,1,0:T(8,128)(2,1)S(1)} %copy-done.7), kind=kOutput, calls=%fused_computation.50 | convolution fusion | flops 1207959552 | bytes 6946816 | tf_op jit(solution)/shard_map/dot_general | solution.py:87
  183.3 10.0 %convolution_convert_fusion = bf16[1152,2048]{1,0:T(8,128)(2,1)} fusion(bf16[1152,2048]{1,0:T(8,128)(2,1)} %bitcast.5, f32[1152,256]{1,0:T(8,128)} %fusion.29, bf16[1,256,2048]{2,1,0:T(8,128)(2,1)} %param.21, bf16[1,2048,256]{2,1,0:T(8,128)(2,1)S(1)} %copy-done), kind=kOutput, calls=%fused_computation.6 | convolution fusion | flops 2420047872 | bytes 12713984 | tf_op jit(solution)/shard_map/dot_general | solution.py:91
  193.3 52.8 %all-to-all-done.2 = bf16[16,72,2048]{2,1,0:T(8,128)(2,1)} async-done(((bf16[16,72,2048]{2,1,0:T(8,128)(2,1)}), bf16[16,72,2048]{2,1,0:T(8,128)(2,1)}, u32[]{:S(2)}, u32[]{:S(2)}) %all-to-all-start.2) | async-done | bytes 4718624 | tf_op jit(solution)/shard_map/all_to_all | solution.py:84
  246.1 7.1 %all-to-all-start.1 = ((bf16[16,72,2048]{2,1,0:T(8,128)(2,1)}), bf16[16,72,2048]{2,1,0:T(8,128)(2,1)}, u32[]{:S(2)}, u32[]{:S(2)}) async-start(bf16[16,72,2048]{2,1,0:T(8,128)(2,1)} %bitcast.91), calls=%async_computation.1 | async-start | bytes 9437184 | tf_op jit(solution)/shard_map/all_to_all | solution.py:121
  253.1 3.7 fusion.27
  256.9 4.2 fusion.21
  261.1 4.5 %multiply_convert_fusion.1 = (bf16[1152,256]{1,0:T(8,128)(2,1)S(1)}, bf16[1152,256]{1,0:T(8,128)(2,1)S(1)}) fusion(f32[1152,256]{1,0:T(8,128)S(1)} %fusion.27, f32[1152,256]{1,0:T(8,128)S(1)} %fusion.21, bf16[1152,2048]{1,0:T(8,128)(2,1)} %bitcast.18, bf16[1,256,2048]{2,1,0:T(8,128)(2,1)S(1)} %copy-done.10), kind=kOutput, calls=%fused_computation.20 | convolution fusion | flops 1211793408 | bytes 9306112 | tf_op jit(solution)/shard_map/rd,hd->rh/dot_general | solution.py:102
  267.1 3.7 fusion
  270.8 49.8 %all-to-all-done.1 = bf16[16,72,2048]{2,1,0:T(8,128)(2,1)} async-done(((bf16[16,72,2048]{2,1,0:T(8,128)(2,1)}), bf16[16,72,2048]{2,1,0:T(8,128)(2,1)}, u32[]{:S(2)}, u32[]{:S(2)}) %all-to-all-start.1) | async-done | bytes 4718624 | tf_op jit(solution)/shard_map/all_to_all | solution.py:121
  320.6 7.2 %all-to-all-start.4 = ((bf16[16,72,2048]{2,1,0:T(8,128)(2,1)}), bf16[16,72,2048]{2,1,0:T(8,128)(2,1)}, u32[]{:S(2)}, u32[]{:S(2)}) async-start(bf16[16,72,2048]{2,1,0:T(8,128)(2,1)} %bitcast.90), calls=%async_computation.4 | async-start | bytes 9437184 | tf_op jit(solution)/shard_map/all_to_all | solution.py:122
  328.0 5.2 %convolution_bitcast_fusion.1 = f32[1,2048,256]{2,1,0:T(8,128)} fusion(bf16[1152,2048]{1,0:T(8,128)(2,1)} %bitcast.22, bf16[1152,256]{1,0:T(8,128)(2,1)S(1)} %get-tuple-element.12), kind=kOutput, calls=%fused_computation.9 | convolution fusion | flops 1207959552 | bytes 7405568 | tf_op jit(solution)/shard_map/rd,rh->dh/dot_general | solution.py:119
  333.3 5.4 %convolution_bitcast_fusion.2 = f32[1,2048,256]{2,1,0:T(8,128)} fusion(bf16[1152,2048]{1,0:T(8,128)(2,1)} %bitcast.22, bf16[1152,256]{1,0:T(8,128)(2,1)S(1)} %get-tuple-element.13), kind=kOutput, calls=%fused_computation.10 | convolution fusion | flops 1207959552 | bytes 7405568 | tf_op jit(solution)/shard_map/rd,rh->dh/dot_general | solution.py:116
  338.6 5.3 %convolution_bitcast_fusion = f32[1,256,2048]{2,1,0:T(8,128)} fusion(bf16[1152,2048]{1,0:T(8,128)(2,1)} %bitcast.18, f32[1152,256]{1,0:T(8,128)S(1)} %copy-done.16, f32[1152,256]{1,0:T(8,128)S(1)} %copy-done.14), kind=kOutput, calls=%fused_computation.8 | convolution fusion | flops 1209729024 | bytes 9175040 | tf_op jit(solution)/shard_map/rh,rd->hd/dot_general | solution.py:120
  354.3 41.1 %all-to-all-done.4 = bf16[16,72,2048]{2,1,0:T(8,128)(2,1)} async-done(((bf16[16,72,2048]{2,1,0:T(8,128)(2,1)}), bf16[16,72,2048]{2,1,0:T(8,128)(2,1)}, u32[]{:S(2)}, u32[]{:S(2)}) %all-to-all-start.4) | async-done | bytes 4718624 | tf_op jit(solution)/shard_map/all_to_all | solution.py:122
  404.7 3.6 reshape.111
  408.3 4.1 multiply_reduce_fusion
  412.3 4.3 %reduce_sum.104 = f32[128,2048]{1,0:T(8,128)S(1)} reduce(f32[128,2,2048]{2,1,0:T(2,128)} %reshape.111, f32[]{:T(128)} %constant.7.clone.1), dimensions={1}, to_apply=%region_8.10 | reduce | flops 262144 | bytes 3145732 | tf_op jit(solution)/shard_map/reduce_sum | solution.py:52
  (71 shorter events, 39.6 us)
Async XLA Ops:
  0.6 182.7 %copy-start = (bf16[1,2048,256]{2,1,0:T(8,128)(2,1)S(1)}, bf16[1,2048,256]{2,1,0:T(8,128)(2,1)}, u32[]{:S(2)}) copy-start(bf16[1,2048,256]{2,1,0:T(8,128)(2,1)} %param.20) | copy-start | bytes 3145732
  7.2 7.7 %copy-start.11 = (bf16[1,128,2048]{2,1,0:T(8,128)(2,1)S(1)}, bf16[1,128,2048]{2,1,0:T(8,128)(2,1)}, u32[]{:S(2)}) copy-start(bf16[1,128,2048]{2,1,0:T(8,128)(2,1)} %param.12) | copy-start | bytes 1572868
  7.2 7.8 %copy-start.8 = (s32[1,128,2]{1,2,0:T(2,128)S(1)}, s32[1,128,2]{1,2,0:T(2,128)}, u32[]{:S(2)}) copy-start(s32[1,128,2]{1,2,0:T(2,128)} %param.15) | copy-start | bytes 3076
  7.2 75.2 %all-to-all-start.3 = ((bf16[16,72,2048]{2,1,0:T(8,128)(2,1)}), bf16[16,72,2048]{2,1,0:T(8,128)(2,1)}, u32[]{:S(2)}, u32[]{:S(2)}) async-start(bf16[16,72,2048]{2,1,0:T(8,128)(2,1)} %bitcast.87), calls=%async_computation.3 | async-start | bytes 9437184 | tf_op jit(solution)/shard_map/all_to_all | solution.py:83
  14.9 22.3 %collective-permute-start = (bf16[1,128,2048]{2,1,0:T(8,128)(2,1)S(1)}, bf16[1,128,2048]{2,1,0:T(8,128)(2,1)S(1)}, u32[]{:S(2)}, u32[]{:S(2)}) collective-permute-start(bf16[1,128,2048]{2,1,0:T(8,128)(2,1)S(1)} %copy-done.11), channel_id=1, source_target_pairs={{0,16},{16,32},{32,48},{48,64},{64,80},{80,96},{96,112},{112,128},... | collective-permute-start | bytes 1572872 | tf_op jit(solution)/shard_map/ppermute | solution.py:13
  37.2 47.9 %copy-start.4 = (bf16[1,128,2048]{2,1,0:T(8,128)(2,1)}, bf16[1,128,2048]{2,1,0:T(8,128)(2,1)S(1)}, u32[]{:S(2)}) copy-start(bf16[1,128,2048]{2,1,0:T(8,128)(2,1)S(1)} %collective-permute-done) | copy-start | bytes 1572868
  85.2 7.2 %copy-start.12 = (bf16[1,128,2048]{2,1,0:T(8,128)(2,1)S(1)}, bf16[1,128,2048]{2,1,0:T(8,128)(2,1)}, u32[]{:S(2)}) copy-start(bf16[1,128,2048]{2,1,0:T(8,128)(2,1)} %param.14) | copy-start | bytes 1572868
  85.2 83.3 %all-to-all-start = ((bf16[16,72,2048]{2,1,0:T(8,128)(2,1)}), bf16[16,72,2048]{2,1,0:T(8,128)(2,1)}, u32[]{:S(2)}, u32[]{:S(2)}) async-start(bf16[16,72,2048]{2,1,0:T(8,128)(2,1)} %bitcast.88), calls=%async_computation | async-start | bytes 9437184 | tf_op jit(solution)/shard_map/all_to_all | solution.py:77
  92.4 26.1 %collective-permute-start.1 = (bf16[1,128,2048]{2,1,0:T(8,128)(2,1)S(1)}, bf16[1,128,2048]{2,1,0:T(8,128)(2,1)S(1)}, u32[]{:S(2)}, u32[]{:S(2)}) collective-permute-start(bf16[1,128,2048]{2,1,0:T(8,128)(2,1)S(1)} %copy-done.12), channel_id=1, source_target_pairs={{0,240},{16,0},{32,16},{48,32},{64,48},{80,64},{96,80},{112,96},{1... | collective-permute-start | bytes 1572872 | tf_op jit(solution)/shard_map/ppermute | solution.py:13
  118.5 0.8 copy-start.5
  171.2 7.4 %copy-start.7 = (bf16[1,2048,256]{2,1,0:T(8,128)(2,1)S(1)}, bf16[1,2048,256]{2,1,0:T(8,128)(2,1)}, u32[]{:S(2)}) copy-start(bf16[1,2048,256]{2,1,0:T(8,128)(2,1)} %param.19) | copy-start | bytes 3145732
  171.2 74.9 %all-to-all-start.2 = ((bf16[16,72,2048]{2,1,0:T(8,128)(2,1)}), bf16[16,72,2048]{2,1,0:T(8,128)(2,1)}, u32[]{:S(2)}, u32[]{:S(2)}) async-start(bf16[16,72,2048]{2,1,0:T(8,128)(2,1)} %bitcast.89), calls=%async_computation.2 | async-start | bytes 9437184 | tf_op jit(solution)/shard_map/all_to_all | solution.py:84
  246.1 74.6 %all-to-all-start.1 = ((bf16[16,72,2048]{2,1,0:T(8,128)(2,1)}), bf16[16,72,2048]{2,1,0:T(8,128)(2,1)}, u32[]{:S(2)}, u32[]{:S(2)}) async-start(bf16[16,72,2048]{2,1,0:T(8,128)(2,1)} %bitcast.91), calls=%async_computation.1 | async-start | bytes 9437184 | tf_op jit(solution)/shard_map/all_to_all | solution.py:121
  256.9 4.2 %copy-start.13 = (f32[1152,256]{1,0:T(8,128)}, f32[1152,256]{1,0:T(8,128)S(1)}, u32[]{:S(2)}) copy-start(f32[1152,256]{1,0:T(8,128)S(1)} %fusion.27) | copy-start | bytes 3538948
  256.9 4.2 %copy-start.10 = (bf16[1,256,2048]{2,1,0:T(8,128)(2,1)S(1)}, bf16[1,256,2048]{2,1,0:T(8,128)(2,1)}, u32[]{:S(2)}) copy-start(bf16[1,256,2048]{2,1,0:T(8,128)(2,1)} %param.21) | copy-start | bytes 3145732
  261.1 4.6 %copy-start.15 = (f32[1152,256]{1,0:T(8,128)}, f32[1152,256]{1,0:T(8,128)S(1)}, u32[]{:S(2)}) copy-start(f32[1152,256]{1,0:T(8,128)S(1)} %fusion.21) | copy-start | bytes 3538948
  320.6 7.2 %copy-start.9 = (f32[1,128,2]{1,2,0:T(2,128)S(1)}, f32[1,128,2]{1,2,0:T(2,128)}, u32[]{:S(2)}) copy-start(f32[1,128,2]{1,2,0:T(2,128)} %param.16) | copy-start | bytes 3076
  320.6 74.7 %all-to-all-start.4 = ((bf16[16,72,2048]{2,1,0:T(8,128)(2,1)}), bf16[16,72,2048]{2,1,0:T(8,128)(2,1)}, u32[]{:S(2)}, u32[]{:S(2)}) async-start(bf16[16,72,2048]{2,1,0:T(8,128)(2,1)} %bitcast.90), calls=%async_computation.4 | async-start | bytes 9437184 | tf_op jit(solution)/shard_map/all_to_all | solution.py:122
  333.2 5.4 %copy-start.14 = (f32[1152,256]{1,0:T(8,128)S(1)}, f32[1152,256]{1,0:T(8,128)}, u32[]{:S(2)}) copy-start(f32[1152,256]{1,0:T(8,128)} %copy-done.13) | copy-start | bytes 3538948
  333.3 5.4 %copy-start.16 = (f32[1152,256]{1,0:T(8,128)S(1)}, f32[1152,256]{1,0:T(8,128)}, u32[]{:S(2)}) copy-start(f32[1152,256]{1,0:T(8,128)} %copy-done.15) | copy-start | bytes 3538948
  404.7 3.6 copy-start.2
  412.3 4.3 %copy-start.3 = (f32[128,2048]{1,0:T(8,128)S(1)}, f32[128,2048]{1,0:T(8,128)}, u32[]{:S(2)}) copy-start(f32[128,2048]{1,0:T(8,128)} %multiply_reduce_fusion) | copy-start | bytes 3145732
  412.3 7.2 %copy-start.1 = (bf16[1,2048,256]{2,1,0:T(8,128)(2,1)S(1)}, bf16[1,2048,256]{2,1,0:T(8,128)(2,1)}, u32[]{:S(2)}) copy-start(bf16[1,2048,256]{2,1,0:T(8,128)(2,1)} %param.20) | copy-start | bytes 3145732
  416.6 2.0 copy-start.6

commit v2 on v0

v2 whole, which is shorter than its diff:
```python
import jax
import jax.numpy as jnp
from jax import lax
from jax.experimental import pallas as pl
from jax.experimental.pallas import tpu as pltpu
from jax.sharding import PartitionSpec as P

E_WIN = 4
TOK = 128
CHIP = 2 * TOK
SLOT = 144
D = 2048
HALF = D // 2
QUART = D // 4
HID = 256
SAVED, FWD, COT = 0, 1, 2
N_COPY = 160
MESH = pl.DeviceIdType.MESH
F32 = jnp.float32
BF16 = jnp.bfloat16


def contract(a, b, dims):
    return lax.dot_general(a, b, ((dims[:1], dims[1:]), ((), ())), preferred_element_type=F32)


def kernel(
    carried, saved, returned, routes, gate_h, up_h, down_h,
    nxt, gin, gate_o, up_o, down_o,
    tok, toky, pack_a, pack_b, rows, gate, up, down, rts, pick, gates,
    keep_f, part_f, sum_in, ret_y, ret_a, ret_b, mix_out, mix_in, fin,
    swish_s, slope_s, hid2_s, pre_s, grad_s, grad_d, ss, rs, ls,
):
    s, r = lax.axis_index("section"), lax.axis_index("expert")
    x, yh, c = r // 4, (r // 2) % 2, r % 2
    oy, oc = 1 - yh, 1 - c
    core_dev = (s, x * 4 + yh * 2 + oc)
    y_dev = (s, x * 4 + oy * 2 + c)
    diag_dev = (s, x * 4 + oy * 2 + oc)

    def x_at(j):
        return lax.rem(x + j, 4)

    def x_dev(j):
        return (s, x_at(j) * 4 + yh * 2 + c)

    def sec_dev(step, dc):
        return (lax.rem(s + step + 16, 16), x * 4 + yh * 2 + lax.rem(c + dc, 2))

    count = [0]
    locals_ = [0]
    pending = []

    def send(src, dst, dev):
        i = count[0]
        count[0] += 1
        copy = pltpu.make_async_remote_copy(
            src_ref=src, dst_ref=dst, send_sem=ss.at[i], recv_sem=rs.at[i], device_id=dev, device_id_type=MESH
        )
        copy.start()
        pending.append(copy)
        return i, copy

    def arrive(i, land, dev):
        pltpu.make_async_remote_copy(
            src_ref=land, dst_ref=land, send_sem=ss.at[i], recv_sem=rs.at[i], device_id=dev, device_id_type=MESH
        ).wait_recv()

    def sent(copy):
        copy.wait_send()
        pending[:] = [other for other in pending if other is not copy]

    def local(src, dst):
        copy = pltpu.make_async_copy(src, dst, ls.at[locals_[0]])
        locals_[0] += 1
        copy.start()
        return copy

    def cols(core, quarter):
        return pl.ds(pl.multiple_of(core * HALF + quarter * QUART, QUART), QUART)

    def half(core):
        return pl.ds(pl.multiple_of(core * HALF, HALF), HALF)

    def lines(core):
        return pl.ds(pl.multiple_of(core * TOK, TOK), TOK)

    barrier = pltpu.get_barrier_semaphore()
    greeted = [core_dev, y_dev, diag_dev, x_dev(1), x_dev(2), x_dev(3), sec_dev(1, 0), sec_dev(1, 1), sec_dev(-1, 0), sec_dev(-1, 1)]
    own_half = local(saved.at[:, half(c)], tok.at[SAVED, lines(c), :])
    weights = [local(gate_h, gate), local(up_h, up), local(down_h, down)]
    for dev in greeted:
        pl.semaphore_signal(barrier, inc=1, device_id=dev, device_id_type=MESH)
    pl.semaphore_wait(barrier, len(greeted))
    i_saved, _ = send(saved.at[:, half(oc)], tok.at[SAVED, lines(c), :], core_dev)
    i_r1, _ = send(routes, rts.at[c], core_dev)
    i_r2, _ = send(routes, rts.at[2 + c], y_dev)
    i_r3, _ = send(routes, rts.at[2 + c], diag_dev)
    i_carry = [send(carried.at[:, half(lax.rem(c + dc, 2))], tok.at[FWD, lines(c), :], sec_dev(1, dc))[0] for dc in (0, 1)]
    i_back = [send(returned.at[:, half(lax.rem(c + dc, 2))], tok.at[COT, lines(c), :], sec_dev(-1, dc))[0] for dc in (0, 1)]
    rts[pl.ds(c, 1)] = routes[...][None]
    arrive(i_r1, rts.at[oc], core_dev)
    arrive(i_r2, rts.at[2 + c], y_dev)
    arrive(i_r3, rts.at[2 + oc], diag_dev)

    expert_of = lax.broadcasted_iota(jnp.int32, (8, CHIP), 0).astype(F32)
    slot_of = lax.broadcasted_iota(jnp.int32, (SLOT, CHIP), 0).astype(F32)
    earlier = (
        lax.broadcasted_iota(jnp.int32, (CHIP, CHIP), 0) < lax.broadcasted_iota(jnp.int32, (CHIP, CHIP), 1)
    ).astype(F32).astype(BF16)

    def table(where, way):
        listed = jnp.concatenate([rts[2 * where], rts[2 * where + 1]], axis=1)
        b = 4 * way
        first, second = listed[b : b + 1] == expert_of, listed[b + 1 : b + 2] == expert_of
        chosen = jnp.logical_or(first, second)
        gates[where, way] = jnp.where(first, listed[b + 2 : b + 3], jnp.where(second, listed[b + 3 : b + 4], 0.0))
        rank = jnp.dot(chosen.astype(F32).astype(BF16), earlier, preferred_element_type=F32)
        rank = jnp.where(chosen, rank, -1.0)
        for e in range(E_WIN):
            pick[where, way, e] = (slot_of == rank[e : e + 1]).astype(F32).astype(BF16)

    def picked(what, where, e, tokens):
        way = 0 if what == FWD else 1
        table_e = pick[where, way, e]
        block = jnp.dot(table_e, tokens, preferred_element_type=F32)
        if what == COT:
            gate_e = gates[where, way, pl.ds(e, 1), :]
            block = block * jnp.sum(table_e.astype(F32) * gate_e, axis=1, keepdims=True)
        return block.astype(BF16)

    ids = {}

    def stage1(t):
        ids[t, "b1"] = send(tok.at[t, :, pl.ds(QUART, QUART)], toky.at[t], y_dev)[0]
        for j in (2, 1, 3, 0):
            block = picked(t, 0, x_at(j), tok[t, :, :QUART])
            if j:
                pack_a[t, j - 1] = block
                ids[t, "xa", j] = send(pack_a.at[t, j - 1], rows.at[t, yh, x, :, cols(c, 0)], x_dev(j))[0]
            else:
                rows[t, yh, x, :, cols(c, 0)] = block

    def stage2(t):
        arrive(ids[t, "b1"], toky.at[t], y_dev)
        for j in (2, 1, 3, 0):
            for where, hh in ((0, yh), (1, oy)):
                tokens = tok[t, :, QUART:] if where == 0 else toky[t]
                block = picked(t, where, x_at(j), tokens)
                if j:
                    pack_b[t, j - 1, hh] = block
                else:
                    rows[t, hh, x, :, cols(c, 1)] = block
            if j:
                ids[t, "xb", j] = send(pack_b.at[t, j - 1], rows.at[t, :, x, :, cols(c, 1)], x_dev(j))[0]
        for j in (0, 1, 3, 2):
            place = rows.at[t, yh, x_at(4 - j), :, cols(c, 0)]
            if j:
                arrive(ids[t, "xa", j], place, x_dev(4 - j))
            ids[t, "ya", j] = send(place, place, y_dev)
        place = rows.at[t, yh, :, :, cols(c, 0)]
        ids[t, "c0"] = send(place, place, core_dev)

    def stage3(t):
        for j in (0, 1, 3, 2):
            arrive(ids[t, "ya", j][0], rows.at[t, oy, x_at(4 - j), :, cols(c, 0)], y_dev)
        place = rows.at[t, oy, :, :, cols(c, 0)]
        ids[t, "c1"] = send(place, place, core_dev)
        for j in (1, 3, 2):
            arrive(ids[t, "xb", j], rows.at[t, :, x_at(4 - j), :, cols(c, 1)], x_dev(4 - j))
        place = rows.at[t, :, :, :, cols(c, 1)]
        ids[t, "c2"] = send(place, place, core_dev)

    def stage4(t):
        arrive(ids[t, "c0"][0], rows.at[t, yh, :, :, cols(oc, 0)], core_dev)
        arrive(ids[t, "c1"][0], rows.at[t, oy, :, :, cols(oc, 0)], core_dev)
        arrive(ids[t, "c2"][0], rows.at[t, :, :, :, cols(oc, 1)], core_dev)

    def group(t, hh):
        return rows[t, hh].reshape(E_WIN * SLOT, D)

    keep = (keep_f, rows.at[FWD, :, :, :, pl.ds(0, HALF)])
    part = (part_f, rows.at[FWD, :, :, :, pl.ds(HALF, HALF)])

    def share(way, hh):
        ids[way, "cs", hh is yh] = send(part[way].at[hh], sum_in.at[way, hh], core_dev)[0]

    def forward(hh):
        token_rows = group(FWD, hh)
        pre_gate = jnp.dot(token_rows, gate[...], preferred_element_type=F32)
        pre_up = jnp.dot(token_rows, up[...], preferred_element_type=F32)
        hidden = (pre_gate * jax.nn.sigmoid(pre_gate) * pre_up).astype(BF16)
        for buffer, core in ((part_f, oc), (keep_f, c)):
            out = jnp.dot(hidden, down[:, half(core)], preferred_element_type=F32)
            buffer[hh] = out.astype(BF16).reshape(E_WIN, SLOT, HALF)
            if core is oc:
                share(0, hh)

    def before(hh):
        token_rows = group(SAVED, hh)
        pre_gate = jnp.dot(token_rows, gate[...], preferred_element_type=F32)
        pre_up = jnp.dot(token_rows, up[...], preferred_element_type=F32)
        sig = jax.nn.sigmoid(pre_gate)
        swish = pre_gate * sig
        swish_s[hh] = swish
        slope_s[hh] = pre_up * sig * (1.0 + pre_gate * (1.0 - sig))
        hid2_s[hh] = (swish * pre_up).astype(BF16)

    def backward(hh):
        grad_hidden = contract(group(COT, hh), down[...], (1, 1))
        grad_gate = (grad_hidden * slope_s[hh]).astype(BF16)
        grad_up = (grad_hidden * swish_s[hh]).astype(BF16)
        pre_s[hh, :, :HID] = grad_gate
        pre_s[hh, :, HID:] = grad_up
        for buffer, core in ((part[1], oc), (keep[1], c)):
            out = contract(grad_gate, gate[half(core), :], (1, 1)) + contract(grad_up, up[half(core), :], (1, 1))
            buffer[hh] = out.astype(BF16).reshape(E_WIN, SLOT, HALF)
            if core is oc:
                share(1, hh)

    def add_core(way, hh):
        arrive(ids[way, "cs", hh is yh], sum_in.at[way, hh], core_dev)
        keep[way][hh] = (keep[way][hh].astype(F32) + sum_in[way, hh].astype(F32)).astype(BF16)

    def return1(way):
        add_core(way, oy)
        ids[way, "ry"] = send(keep[way].at[oy, :, :, pl.ds(0, QUART)], ret_y.at[way], y_dev)[0]
        add_core(way, yh)
        for j in (2, 1, 3):
            ids[way, "rb", j] = send(keep[way].at[:, x_at(j), :, pl.ds(QUART, QUART)], ret_b.at[way, :, x], x_dev(j))[0]
        ret_b[way, :, x] = keep[way][:, x, :, QUART:]

    def return2(way):
        arrive(ids[way, "ry"], ret_y.at[way], y_dev)
        both = keep[way][yh, :, :, :QUART].astype(F32) + ret_y[way].astype(F32)
        keep[way][yh, :, :, :QUART] = both.astype(BF16)
        for j in (2, 1, 3):
            ids[way, "ra", j] = send(keep[way].at[yh, x_at(j), :, pl.ds(0, QUART)], ret_a.at[way, x], x_dev(j))[0]
        ret_a[way, x] = keep[way][yh, x, :, :QUART]

    def mixed(way, where, block):
        block = block.reshape(E_WIN * SLOT, QUART)
        table_all = pick[where, way].astype(F32)
        if way == 1:
            return contract(table_all.reshape(E_WIN * SLOT, CHIP).astype(BF16), block, (0, 0))
        weight = gates[where, way][:E_WIN]
        coarse = weight.astype(BF16).astype(F32)
        fine = weight - coarse
        coarse = (table_all * coarse[:, None, :]).reshape(E_WIN * SLOT, CHIP).astype(BF16)
        fine = (table_all * fine[:, None, :]).reshape(E_WIN * SLOT, CHIP).astype(BF16)
        return contract(coarse, block, (0, 0)) + contract(fine, block, (0, 0))

    def return3(way):
        t = FWD if way == 0 else COT
        for j in (1, 3, 2):
            arrive(ids[way, "rb", j], ret_b.at[way, :, x_at(4 - j)], x_dev(4 - j))
        mix_out[way] = mixed(way, 1, ret_b[way, oy]).astype(BF16)
        i = send(mix_out.at[way], mix_in.at[way], y_dev)[0]
        total = tok[t, :, QUART:].astype(F32) + mixed(way, 0, ret_b[way, yh])
        for j in (1, 3, 2):
            arrive(ids[way, "ra", j], ret_a.at[way, x_at(4 - j)], x_dev(4 - j))
        fin[way, :, :QUART] = (tok[t, :, :QUART].astype(F32) + mixed(way, 0, ret_a[way])).astype(BF16)
        arrive(i, mix_in.at[way], y_dev)
        fin[way, :, QUART:] = (total + mix_in[way].astype(F32)).astype(BF16)
        out = (nxt, gin)[way]
        ids[way, "out"] = send(fin.at[way, lines(oc), :], out.at[:, half(c)], core_dev)[0]
        ids[way, "mine"] = local(fin.at[way, lines(c), :], out.at[:, half(c)])

    def weight_grads():
        step = 512

        def one(k, carry):
            place = pl.ds(pl.multiple_of(k * step, step), step)
            lhs = rows[SAVED, :, :, :, place].reshape(2 * E_WIN * SLOT, step)
            grad_s[place, :] = contract(lhs, pre_s[...].reshape(2 * E_WIN * SLOT, 2 * HID), (0, 0))
            rhs = rows[COT, :, :, :, place].reshape(2 * E_WIN * SLOT, step)
            grad_d[:, place] = contract(hid2_s[...].reshape(2 * E_WIN * SLOT, HID), rhs, (0, 0))
            return carry

        lax.fori_loop(0, D // step, one, 0)
        return [local(grad_s.at[:, pl.ds(0, HID)], gate_o), local(grad_s.at[:, pl.ds(HID, HID)], up_o), local(grad_d, down_o)]

    table(0, 1)
    own_half.wait()
    arrive(i_saved, tok.at[SAVED, lines(oc), :], core_dev)
    stage1(SAVED)
    table(1, 1)
    table(0, 0)
    table(1, 0)
    stage2(SAVED)
    for dc in (0, 1):
        arrive(i_carry[dc], tok.at[FWD, lines(lax.rem(c + dc, 2)), :], sec_dev(-1, dc))
    stage1(FWD)
    stage3(SAVED)
    stage2(FWD)
    for copy in weights:
        copy.wait()
    stage4(SAVED)
    before(oy)
    before(yh)
    for dc in (0, 1):
        arrive(i_back[dc], tok.at[COT, lines(lax.rem(c + dc, 2)), :], sec_dev(1, dc))
    stage1(COT)
    stage3(FWD)
    stage2(COT)
    stage4(FWD)
    forward(oy)
    forward(yh)
    return1(0)
    return2(0)
    stage3(COT)
    stage4(COT)
    for key in [("c0"), ("c1"), ("c2")]:
        sent(ids[FWD, key][1])
    for j in range(4):
        sent(ids[FWD, "ya", j][1])
    backward(oy)
    backward(yh)
    return1(1)
    return2(1)
    return3(0)
    grads_out = weight_grads()
    return3(1)
    for way, out in ((0, nxt), (1, gin)):
        arrive(ids[way, "out"], out.at[:, half(oc)], core_dev)
        ids[way, "mine"].wait()
    for copy in grads_out:
        copy.wait()
    for copy in list(pending):
        copy.wait_send()


def body(carried, saved_rows, returned, fwd_ids, fwd_gates, bwd_ids, bwd_gates, gate_w, up_w, down_w):
    routes = jnp.concatenate([fwd_ids[0].astype(F32), fwd_gates[0], bwd_ids[0].astype(F32), bwd_gates[0]], axis=1).T
    whole = pl.BlockSpec(memory_space=pl.ANY)
    group_rows = E_WIN * SLOT
    scratch = [
        pltpu.VMEM((3, CHIP, HALF), BF16),
        pltpu.VMEM((3, CHIP, QUART), BF16),
        pltpu.VMEM((3, 3, SLOT, QUART), BF16),
        pltpu.VMEM((3, 3, 2, SLOT, QUART), BF16),
        pltpu.VMEM((3, 2, E_WIN, SLOT, D), BF16),
        pltpu.VMEM((D, HID), BF16),
        pltpu.VMEM((D, HID), BF16),
        pltpu.VMEM((HID, D), BF16),
        pltpu.VMEM((4, 8, TOK), F32),
        pltpu.VMEM((2, 2, E_WIN, SLOT, CHIP), BF16),
        pltpu.VMEM((2, 2, 8, CHIP), F32),
        pltpu.VMEM((2, E_WIN, SLOT, HALF), BF16),
        pltpu.VMEM((2, E_WIN, SLOT, HALF), BF16),
        pltpu.VMEM((2, 2, E_WIN, SLOT, HALF), BF16),
        pltpu.VMEM((2, E_WIN, SLOT, QUART), BF16),
        pltpu.VMEM((2, E_WIN, SLOT, QUART), BF16),
        pltpu.VMEM((2, 2, E_WIN, SLOT, QUART), BF16),
        pltpu.VMEM((2, CHIP, QUART), BF16),
        pltpu.VMEM((2, CHIP, QUART), BF16),
        pltpu.VMEM((2, CHIP, HALF), BF16),
        pltpu.VMEM((2, group_rows, HID), F32),
        pltpu.VMEM((2, group_rows, HID), F32),
        pltpu.VMEM((2, group_rows, HID), BF16),
        pltpu.VMEM((2, group_rows, 2 * HID), BF16),
        pltpu.VMEM((D, 2 * HID), F32),
        pltpu.VMEM((HID, D), F32),
        pltpu.SemaphoreType.DMA((N_COPY,)),
        pltpu.SemaphoreType.DMA((N_COPY,)),
        pltpu.SemaphoreType.DMA((16,)),
    ]
    rows_all = 2 * group_rows
    outs = pl.pallas_call(
        kernel,
        name="relay_tick",
        out_shape=(
            jax.ShapeDtypeStruct((TOK, D), BF16),
            jax.ShapeDtypeStruct((TOK, D), BF16),
            jax.ShapeDtypeStruct((D, HID), F32),
            jax.ShapeDtypeStruct((D, HID), F32),
            jax.ShapeDtypeStruct((HID, D), F32),
        ),
        in_specs=[whole] * 3 + [pl.BlockSpec(memory_space=pltpu.VMEM)] + [whole] * 3,
        out_specs=(whole,) * 5,
        scratch_shapes=scratch,
        compiler_params=pltpu.CompilerParams(collective_id=0, has_side_effects=True, vmem_limit_bytes=60 * 2**20),
        cost_estimate=pl.CostEstimate(flops=2 * rows_all * D * 2816, bytes_accessed=12 * 2**20, transcendentals=2 * rows_all * HID),
    )(carried[0], saved_rows[0], returned[0], routes, gate_w[0], up_w[0], down_w[0])
    return tuple(out[None] for out in outs)


def solution(mesh):
    tokens = P("section", "expert", None)
    columns = P("section", None, "expert")
    return jax.shard_map(
        body,
        mesh=mesh,
        in_specs=(tokens,) * 7 + (columns, columns, tokens),
        out_specs=(tokens, tokens, columns, columns, tokens),
        check_vma=False,
    )
```

time: 422 us -> 167 us (0.40)
  the two profiles are of different devices: /device:TPU:245 before, /device:TPU:1 now
where the time goes in v2:
time: 167 us
  Pallas kernels  154 us (92%)
  local copies, waits for them, and re-layouts  9.93 us (6%)
  other arithmetic  2 us (1%)
    pallas_call x1, Pallas kernels, body(): pl.pallas_call(kernel, name='relay_tick', out_shape=(jax.ShapeDtypeStruct...  154 us
    unnamed x11, local copies, waits for them, and re-layouts  9.93 us

profile of v2, /device:TPU:1, one launch (start us, length us, event | category | flops | bytes accessed | tf_op | source)
XLA Modules:
  0.0 166.8 jit_solution(8746544121843252807)
XLA Ops:
  0.6 0.7 convert_bitcast_fusion
  1.3 1.3 maximum_bitcast_fusion.routes
  2.6 154.3 %relay_tick.1 = (bf16[128,2048]{1,0:T(8,128)(2,1)}, bf16[128,2048]{1,0:T(8,128)(2,1)}, f32[2048,256]{1,0:T(8,128)}, f32[2048,256]{1,0:T(8,128)}, f32[256,2048]{1,0:T(8,128)}) custom-call(bf16[128,2048]{1,0:T(8,128)(2,1)} %bitcast.29, bf16[128,2048]{1,0:T(8,128)(2,1)} %bitcast.30, bf16[128,2048]{1,0:T(8,128)(2,1)} %bitcast.31, ...), custom_call_target="tpu_custom_call" | custom-call | flops 13287555072 | bytes 12582912 | tf_op jit(solution)/shard_map/relay_tick/pallas_call | solution.py:369
  156.9 0.0 copy-start.2
  156.9 2.0 %copy.20 = bf16[1,128,2048]{2,1,0:T(8,128)(2,1)} copy(bf16[1,128,2048]{2,1,0:T(8,128)(2,1)} %bitcast.23) | data formatting | bytes 1048576
  158.9 1.9 %copy.21 = bf16[1,128,2048]{2,1,0:T(8,128)(2,1)} copy(bf16[1,128,2048]{2,1,0:T(8,128)(2,1)} %bitcast.22) | data formatting | bytes 1048576
  160.8 0.0 copy-done.2
  160.8 0.0 copy-start.1
  160.8 1.3 copy.22
  162.1 1.0 copy-done.1
  163.2 0.0 copy-start
  163.2 1.3 copy.23
  164.5 1.0 copy-done
  165.5 1.3 copy.24
Async XLA Ops:
  156.9 3.9 %copy-start.2 = (f32[2048,256]{1,0:T(8,128)S(1)}, f32[2048,256]{1,0:T(8,128)}, u32[]{:S(2)}) copy-start(f32[2048,256]{1,0:T(8,128)} %get-tuple-element.12) | copy-start | bytes 6291460
  160.8 2.3 %copy-start.1 = (f32[2048,256]{1,0:T(8,128)S(1)}, f32[2048,256]{1,0:T(8,128)}, u32[]{:S(2)}) copy-start(f32[2048,256]{1,0:T(8,128)} %get-tuple-element.13) | copy-start | bytes 6291460
  163.2 2.3 %copy-start = (f32[256,2048]{1,0:T(8,128)S(1)}, f32[256,2048]{1,0:T(8,128)}, u32[]{:S(2)}) copy-start(f32[256,2048]{1,0:T(8,128)} %get-tuple-element.14) | copy-start | bytes 6291460

commit v3 on v2

--- a/solution.py
+++ b/solution.py
@@ -25,11 +25,11 @@
 
 
 def kernel(
-    carried, saved, returned, routes, gate_h, up_h, down_h,
+    carried, saved, returned, fwd_ids, fwd_gates, bwd_ids, bwd_gates, gate_h, up_h, down_h,
     nxt, gin, gate_o, up_o, down_o,
-    tok, toky, pack_a, pack_b, rows, gate, up, down, rts, pick, gates,
-    keep_f, part_f, sum_in, ret_y, ret_a, ret_b, mix_out, mix_in, fin,
-    swish_s, slope_s, hid2_s, pre_s, grad_s, grad_d, ss, rs, ls,
+    tok, toky, pack_a, pack_b, rows, gate, up, down, routes, rts, pick, gates,
+    keep_b, part_b, sum_in, ret_y, ret_a, ret_b, mix_out, mix_in, fin,
+    swish_s, slope_s, hid2_s, pre_s, ss, rs, ls,
 ):
     s, r = lax.axis_index("section"), lax.axis_index("expert")
     x, yh, c = r // 4, (r // 2) % 2, r % 2
@@ -89,19 +89,22 @@
     greeted = [core_dev, y_dev, diag_dev, x_dev(1), x_dev(2), x_dev(3), sec_dev(1, 0), sec_dev(1, 1), sec_dev(-1, 0), sec_dev(-1, 1)]
     own_half = local(saved.at[:, half(c)], tok.at[SAVED, lines(c), :])
     weights = [local(gate_h, gate), local(up_h, up), local(down_h, down)]
+    for row, numbers in enumerate((fwd_ids, fwd_gates, bwd_ids, bwd_gates)):
+        routes[2 * row : 2 * row + 2, :] = numbers[...].astype(F32)
     for dev in greeted:
         pl.semaphore_signal(barrier, inc=1, device_id=dev, device_id_type=MESH)
     pl.semaphore_wait(barrier, len(greeted))
-    i_saved, _ = send(saved.at[:, half(oc)], tok.at[SAVED, lines(c), :], core_dev)
     i_r1, _ = send(routes, rts.at[c], core_dev)
     i_r2, _ = send(routes, rts.at[2 + c], y_dev)
     i_r3, _ = send(routes, rts.at[2 + c], diag_dev)
+    i_saved, _ = send(saved.at[:, half(oc)], tok.at[SAVED, lines(c), :], core_dev)
+    i_b1 = [
+        send(saved.at[:, cols(c, 1)], toky.at[SAVED, lines(c), :], y_dev)[0],
+        send(saved.at[:, cols(oc, 1)], toky.at[SAVED, lines(c), :], diag_dev)[0],
+    ]
+    i_back = [send(returned.at[:, half(lax.rem(c + dc, 2))], tok.at[COT, lines(c), :], sec_dev(-1, dc))[0] for dc in (0, 1)]
     i_carry = [send(carried.at[:, half(lax.rem(c + dc, 2))], tok.at[FWD, lines(c), :], sec_dev(1, dc))[0] for dc in (0, 1)]
-    i_back = [send(returned.at[:, half(lax.rem(c + dc, 2))], tok.at[COT, lines(c), :], sec_dev(-1, dc))[0] for dc in (0, 1)]
     rts[pl.ds(c, 1)] = routes[...][None]
-    arrive(i_r1, rts.at[oc], core_dev)
-    arrive(i_r2, rts.at[2 + c], y_dev)
-    arrive(i_r3, rts.at[2 + oc], diag_dev)
 
     expert_of = lax.broadcasted_iota(jnp.int32, (8, CHIP), 0).astype(F32)
     slot_of = lax.broadcasted_iota(jnp.int32, (SLOT, CHIP), 0).astype(F32)
@@ -132,7 +135,8 @@
     ids = {}
 
     def stage1(t):
-        ids[t, "b1"] = send(tok.at[t, :, pl.ds(QUART, QUART)], toky.at[t], y_dev)[0]
+        if t != SAVED:
+            ids[t, "b1"] = send(tok.at[t, :, pl.ds(QUART, QUART)], toky.at[t], y_dev)[0]
         for j in (2, 1, 3, 0):
             block = picked(t, 0, x_at(j), tok[t, :, :QUART])
             if j:
@@ -142,7 +146,11 @@
                 rows[t, yh, x, :, cols(c, 0)] = block
 
     def stage2(t):
-        arrive(ids[t, "b1"], toky.at[t], y_dev)
+        if t == SAVED:
+            arrive(i_b1[0], toky.at[t, lines(c), :], y_dev)
+            arrive(i_b1[1], toky.at[t, lines(oc), :], diag_dev)
+        else:
+            arrive(ids[t, "b1"], toky.at[t], y_dev)
         for j in (2, 1, 3, 0):
             for where, hh in ((0, yh), (1, oy)):
                 tokens = tok[t, :, QUART:] if where == 0 else toky[t]
@@ -179,8 +187,8 @@
     def group(t, hh):
         return rows[t, hh].reshape(E_WIN * SLOT, D)
 
-    keep = (keep_f, rows.at[FWD, :, :, :, pl.ds(0, HALF)])
-    part = (part_f, rows.at[FWD, :, :, :, pl.ds(HALF, HALF)])
+    keep = (rows.at[FWD, :, :, :, pl.ds(0, HALF)], keep_b)
+    part = (rows.at[FWD, :, :, :, pl.ds(HALF, HALF)], part_b)
 
     def share(way, hh):
         ids[way, "cs", hh is yh] = send(part[way].at[hh], sum_in.at[way, hh], core_dev)[0]
@@ -190,7 +198,7 @@
         pre_gate = jnp.dot(token_rows, gate[...], preferred_element_type=F32)
         pre_up = jnp.dot(token_rows, up[...], preferred_element_type=F32)
         hidden = (pre_gate * jax.nn.sigmoid(pre_gate) * pre_up).astype(BF16)
-        for buffer, core in ((part_f, oc), (keep_f, c)):
+        for buffer, core in ((part[0], oc), (keep[0], c)):
             out = jnp.dot(hidden, down[:, half(core)], preferred_element_type=F32)
             buffer[hh] = out.astype(BF16).reshape(E_WIN, SLOT, HALF)
             if core is oc:
@@ -223,12 +231,15 @@
         keep[way][hh] = (keep[way][hh].astype(F32) + sum_in[way, hh].astype(F32)).astype(BF16)
 
     def return1(way):
-        add_core(way, oy)
-        ids[way, "ry"] = send(keep[way].at[oy, :, :, pl.ds(0, QUART)], ret_y.at[way], y_dev)[0]
-        add_core(way, yh)
-        for j in (2, 1, 3):
-            ids[way, "rb", j] = send(keep[way].at[:, x_at(j), :, pl.ds(QUART, QUART)], ret_b.at[way, :, x], x_dev(j))[0]
-        ret_b[way, :, x] = keep[way][:, x, :, QUART:]
+        for where, hh in ((1, oy), (0, yh)):
+            add_core(way, hh)
+            if where:
+                ids[way, "ry"] = send(keep[way].at[oy, :, :, pl.ds(0, QUART)], ret_y.at[way], y_dev)[0]
+            for j in (2, 1, 3):
+                ids[way, "rb", where, j] = send(
+                    keep[way].at[hh, x_at(j), :, pl.ds(QUART, QUART)], ret_b.at[way, hh, x], x_dev(j)
+                )[0]
+            ret_b[way, hh, x] = keep[way][hh, x, :, QUART:]
 
     def return2(way):
         arrive(ids[way, "ry"], ret_y.at[way], y_dev)
@@ -251,17 +262,21 @@
         return contract(coarse, block, (0, 0)) + contract(fine, block, (0, 0))
 
     def return3(way):
+        for j in (1, 3, 2):
+            arrive(ids[way, "rb", 1, j], ret_b.at[way, oy, x_at(4 - j)], x_dev(4 - j))
+        mix_out[way] = mixed(way, 1, ret_b[way, oy]).astype(BF16)
+        ids[way, "uy"] = send(mix_out.at[way], mix_in.at[way], y_dev)[0]
+
+    def return4(way):
         t = FWD if way == 0 else COT
         for j in (1, 3, 2):
-            arrive(ids[way, "rb", j], ret_b.at[way, :, x_at(4 - j)], x_dev(4 - j))
-        mix_out[way] = mixed(way, 1, ret_b[way, oy]).astype(BF16)
-        i = send(mix_out.at[way], mix_in.at[way], y_dev)[0]
+            arrive(ids[way, "rb", 0, j], ret_b.at[way, yh, x_at(4 - j)], x_dev(4 - j))
         total = tok[t, :, QUART:].astype(F32) + mixed(way, 0, ret_b[way, yh])
+        arrive(ids[way, "uy"], mix_in.at[way], y_dev)
+        fin[way, :, QUART:] = (total + mix_in[way].astype(F32)).astype(BF16)
         for j in (1, 3, 2):
             arrive(ids[way, "ra", j], ret_a.at[way, x_at(4 - j)], x_dev(4 - j))
         fin[way, :, :QUART] = (tok[t, :, :QUART].astype(F32) + mixed(way, 0, ret_a[way])).astype(BF16)
-        arrive(i, mix_in.at[way], y_dev)
-        fin[way, :, QUART:] = (total + mix_in[way].astype(F32)).astype(BF16)
         out = (nxt, gin)[way]
         ids[way, "out"] = send(fin.at[way, lines(oc), :], out.at[:, half(c)], core_dev)[0]
         ids[way, "mine"] = local(fin.at[way, lines(c), :], out.at[:, half(c)])
@@ -272,66 +287,79 @@
         def one(k, carry):
             place = pl.ds(pl.multiple_of(k * step, step), step)
             lhs = rows[SAVED, :, :, :, place].reshape(2 * E_WIN * SLOT, step)
-            grad_s[place, :] = contract(lhs, pre_s[...].reshape(2 * E_WIN * SLOT, 2 * HID), (0, 0))
+            both = contract(lhs, pre_s[...].reshape(2 * E_WIN * SLOT, 2 * HID), (0, 0))
+            gate_o[place, :] = both[:, :HID]
+            up_o[place, :] = both[:, HID:]
             rhs = rows[COT, :, :, :, place].reshape(2 * E_WIN * SLOT, step)
-            grad_d[:, place] = contract(hid2_s[...].reshape(2 * E_WIN * SLOT, HID), rhs, (0, 0))
+            down_o[:, place] = contract(hid2_s[...].reshape(2 * E_WIN * SLOT, HID), rhs, (0, 0))
             return carry
 
         lax.fori_loop(0, D // step, one, 0)
-        return [local(grad_s.at[:, pl.ds(0, HID)], gate_o), local(grad_s.at[:, pl.ds(HID, HID)], up_o), local(grad_d, down_o)]
-
+
+    arrive(i_r1, rts.at[oc], core_dev)
     table(0, 1)
     own_half.wait()
     arrive(i_saved, tok.at[SAVED, lines(oc), :], core_dev)
     stage1(SAVED)
+    arrive(i_r2, rts.at[2 + c], y_dev)
+    arrive(i_r3, rts.at[2 + oc], diag_dev)
     table(1, 1)
     table(0, 0)
     table(1, 0)
     stage2(SAVED)
     for dc in (0, 1):
+        arrive(i_back[dc], tok.at[COT, lines(lax.rem(c + dc, 2)), :], sec_dev(1, dc))
+    stage1(COT)
+    for dc in (0, 1):
         arrive(i_carry[dc], tok.at[FWD, lines(lax.rem(c + dc, 2)), :], sec_dev(-1, dc))
     stage1(FWD)
-    stage3(SAVED)
-    stage2(FWD)
     for copy in weights:
         copy.wait()
+    stage3(SAVED)
     stage4(SAVED)
     before(oy)
+    stage2(COT)
     before(yh)
-    for dc in (0, 1):
-        arrive(i_back[dc], tok.at[COT, lines(lax.rem(c + dc, 2)), :], sec_dev(1, dc))
-    stage1(COT)
+    stage2(FWD)
+    stage3(COT)
+    stage4(COT)
+    backward(oy)
+    backward(yh)
+    return1(1)
     stage3(FWD)
-    stage2(COT)
     stage4(FWD)
+    for key in ("c0", "c1", "c2"):
+        sent(ids[FWD, key][1])
+    for j in range(4):
+        sent(ids[FWD, "ya", j][1])
     forward(oy)
     forward(yh)
     return1(0)
+    weight_grads()
+    return2(1)
+    return3(1)
+    return3(0)
     return2(0)
-    stage3(COT)
-    stage4(COT)
-    for key in [("c0"), ("c1"), ("c2")]:
-        sent(ids[FWD, key][1])
-    for j in range(4):
-        sent(ids[FWD, "ya", j][1])
-    backward(oy)
-    backward(yh)
-    return1(1)
-    return2(1)
-    return3(0)
-    grads_out = weight_grads()
-    return3(1)
+    return4(1)
+    return4(0)
     for way, out in ((0, nxt), (1, gin)):
         arrive(ids[way, "out"], out.at[:, half(oc)], core_dev)
         ids[way, "mine"].wait()
-    for copy in grads_out:
-        copy.wait()
     for copy in list(pending):
         copy.wait_send()
 
 
+def write_out(*refs):
+    ins, outs, sem = refs[:5], refs[5:10], refs[10]
+    copies = [pltpu.make_async_copy(a, b, sem.at[i]) for i, (a, b) in enumerate(zip(ins, outs))]
+    for copy in copies:
+        copy.start()
+    for copy in copies:
+        copy.wait()
+
+
 def body(carried, saved_rows, returned, fwd_ids, fwd_gates, bwd_ids, bwd_gates, gate_w, up_w, down_w):
-    routes = jnp.concatenate([fwd_ids[0].astype(F32), fwd_gates[0], bwd_ids[0].astype(F32), bwd_gates[0]], axis=1).T
+    routes = [numbers[0].T for numbers in (fwd_ids, fwd_gates, bwd_ids, bwd_gates)]
     whole = pl.BlockSpec(memory_space=pl.ANY)
     group_rows = E_WIN * SLOT
     scratch = [
@@ -343,6 +371,7 @@
         pltpu.VMEM((D, HID), BF16),
         pltpu.VMEM((D, HID), BF16),
         pltpu.VMEM((HID, D), BF16),
+        pltpu.VMEM((8, TOK), F32),
         pltpu.VMEM((4, 8, TOK), F32),
         pltpu.VMEM((2, 2, E_WIN, SLOT, CHIP), BF16),
         pltpu.VMEM((2, 2, 8, CHIP), F32),
@@ -359,29 +388,32 @@
         pltpu.VMEM((2, group_rows, HID), F32),
         pltpu.VMEM((2, group_rows, HID), BF16),
         pltpu.VMEM((2, group_rows, 2 * HID), BF16),
-        pltpu.VMEM((D, 2 * HID), F32),
-        pltpu.VMEM((HID, D), F32),
         pltpu.SemaphoreType.DMA((N_COPY,)),
         pltpu.SemaphoreType.DMA((N_COPY,)),
         pltpu.SemaphoreType.DMA((16,)),
     ]
     rows_all = 2 * group_rows
+    vmem = pl.BlockSpec(memory_space=pltpu.VMEM)
+    results = [((TOK, D), BF16)] * 2 + [((D, HID), F32)] * 2 + [((HID, D), F32)]
     outs = pl.pallas_call(
         kernel,
         name="relay_tick",
-        out_shape=(
-            jax.ShapeDtypeStruct((TOK, D), BF16),
-            jax.ShapeDtypeStruct((TOK, D), BF16),
-            jax.ShapeDtypeStruct((D, HID), F32),
-            jax.ShapeDtypeStruct((D, HID), F32),
-            jax.ShapeDtypeStruct((HID, D), F32),
-        ),
-        in_specs=[whole] * 3 + [pl.BlockSpec(memory_space=pltpu.VMEM)] + [whole] * 3,
+        out_shape=tuple(pltpu.VMEM(shape, dtype) for shape, dtype in results),
+        in_specs=[whole] * 3 + [vmem] * 4 + [whole] * 3,
+        out_specs=(vmem,) * 5,
+        scratch_shapes=scratch,
+        compiler_params=pltpu.CompilerParams(collective_id=0, has_side_effects=True, vmem_limit_bytes=53 * 2**20),
+        cost_estimate=pl.CostEstimate(flops=2 * rows_all * D * 2816, bytes_accessed=12 * 2**20, transcendentals=2 * rows_all * HID),
+    )(carried[0], saved_rows[0], returned[0], *routes, gate_w[0], up_w[0], down_w[0])
+    outs = pl.pallas_call(
+        write_out,
+        name="write_out",
+        out_shape=tuple(jax.ShapeDtypeStruct(shape, dtype) for shape, dtype in results),
+        in_specs=[vmem] * 5,
         out_specs=(whole,) * 5,
-        scratch_shapes=scratch,
-        compiler_params=pltpu.CompilerParams(collective_id=0, has_side_effects=True, vmem_limit_bytes=60 * 2**20),
-        cost_estimate=pl.CostEstimate(flops=2 * rows_all * D * 2816, bytes_accessed=12 * 2**20, transcendentals=2 * rows_all * HID),
-    )(carried[0], saved_rows[0], returned[0], routes, gate_w[0], up_w[0], down_w[0])
+        scratch_shapes=[pltpu.SemaphoreType.DMA((5,))],
+        compiler_params=pltpu.CompilerParams(vmem_limit_bytes=2**20),
+    )(*outs)
     return tuple(out[None] for out in outs)
 
 

time: 167 us -> 132 us (0.79)
  Pallas kernels: 154 us -> 131 us
  local copies, waits for them, and re-layouts: 9.93 us -> 0 us
  other arithmetic: 2 us -> 0 us
    pallas_call x1 -> x2, Pallas kernels: 154 us -> 131 us  [the longest x1 128 us: body(): pl.pallas_call(kernel, name='relay_tick', out_shape=tuple((pltpu.VMEM(sha...]
    unnamed x11 -> x0, local copies, waits for them, and re-layouts: 9.93 us -> none
where the time goes in v3:
time: 132 us; the launch traced here: 131 us
  Pallas kernels  131 us (99%)
    pallas_call x1, Pallas kernels, body(): pl.pallas_call(kernel, name='relay_tick', out_shape=tuple((pltpu.VMEM(sha...  128 us
    pallas_call x1, Pallas kernels, body(): pl.pallas_call(write_out, name='write_out', out_shape=tuple((jax.ShapeDty...  3.09 us

profile of v3, /device:TPU:1, one launch (start us, length us, event | category | flops | bytes accessed | tf_op | source)
XLA Modules:
  0.0 131.5 jit_solution(3575736073344478633)
XLA Ops:
  0.6 127.6 %relay_tick.1 = (bf16[128,2048]{1,0:T(8,128)(2,1)S(1)}, bf16[128,2048]{1,0:T(8,128)(2,1)S(1)}, f32[2048,256]{1,0:T(8,128)S(1)}, f32[2048,256]{1,0:T(8,128)S(1)}, f32[256,2048]{1,0:T(8,128)S(1)}) custom-call(bf16[128,2048]{1,0:T(8,128)(2,1)} %bitcast.29, bf16[128,2048]{1,0:T(8,128)(2,1)} %bitcast.30, bf16[128,2048]{1,0:T(8,128)(2,1)} %bitcast.31, ...), custom_call_target="tpu_custom_call" | custom-call | flops 13287555072 | bytes 12582912 | tf_op jit(solution)/shard_map/relay_tick/pallas_call | solution.py:398
  128.2 3.1 %write_out.1 = (bf16[128,2048]{1,0:T(8,128)(2,1)}, bf16[128,2048]{1,0:T(8,128)(2,1)}, f32[2048,256]{1,0:T(8,128)}, f32[2048,256]{1,0:T(8,128)}, f32[256,2048]{1,0:T(8,128)}) custom-call(bf16[128,2048]{1,0:T(8,128)(2,1)S(1)} %get-tuple-element.15.refs_0_, bf16[128,2048]{1,0:T(8,128)(2,1)S(1)} %get-tuple-element.16.refs_1_, ...), custom_call_target="tpu_custom_call" | custom-call | tf_op jit(solution)/shard_map/write_out/pallas_call | solution.py:408

commit v4 on v3

--- a/solution.py
+++ b/solution.py
@@ -14,7 +14,7 @@
 QUART = D // 4
 HID = 256
 SAVED, FWD, COT = 0, 1, 2
-N_COPY = 160
+N_COPY = 79
 MESH = pl.DeviceIdType.MESH
 F32 = jnp.float32
 BF16 = jnp.bfloat16
@@ -249,34 +249,40 @@
             ids[way, "ra", j] = send(keep[way].at[yh, x_at(j), :, pl.ds(0, QUART)], ret_a.at[way, x], x_dev(j))[0]
         ret_a[way, x] = keep[way][yh, x, :, :QUART]
 
-    def mixed(way, where, block):
-        block = block.reshape(E_WIN * SLOT, QUART)
-        table_all = pick[where, way].astype(F32)
+    def mixed(way, where, e, block):
+        table_e = pick[where, way, e]
         if way == 1:
-            return contract(table_all.reshape(E_WIN * SLOT, CHIP).astype(BF16), block, (0, 0))
-        weight = gates[where, way][:E_WIN]
+            return contract(table_e, block, (0, 0))
+        weight = gates[where, way, pl.ds(e, 1), :]
         coarse = weight.astype(BF16).astype(F32)
-        fine = weight - coarse
-        coarse = (table_all * coarse[:, None, :]).reshape(E_WIN * SLOT, CHIP).astype(BF16)
-        fine = (table_all * fine[:, None, :]).reshape(E_WIN * SLOT, CHIP).astype(BF16)
-        return contract(coarse, block, (0, 0)) + contract(fine, block, (0, 0))
+        wide = table_e.astype(F32)
+        parts = [(wide * part_of).astype(BF16) for part_of in (coarse, weight - coarse)]
+        return contract(parts[0], block, (0, 0)) + contract(parts[1], block, (0, 0))
 
     def return3(way):
+        total = mixed(way, 1, x, ret_b[way, oy, x])
         for j in (1, 3, 2):
-            arrive(ids[way, "rb", 1, j], ret_b.at[way, oy, x_at(4 - j)], x_dev(4 - j))
-        mix_out[way] = mixed(way, 1, ret_b[way, oy]).astype(BF16)
+            e = x_at(4 - j)
+            arrive(ids[way, "rb", 1, j], ret_b.at[way, oy, e], x_dev(4 - j))
+            total = total + mixed(way, 1, e, ret_b[way, oy, e])
+        mix_out[way] = total.astype(BF16)
         ids[way, "uy"] = send(mix_out.at[way], mix_in.at[way], y_dev)[0]
 
     def return4(way):
         t = FWD if way == 0 else COT
+        total = tok[t, :, QUART:].astype(F32) + mixed(way, 0, x, ret_b[way, yh, x])
         for j in (1, 3, 2):
-            arrive(ids[way, "rb", 0, j], ret_b.at[way, yh, x_at(4 - j)], x_dev(4 - j))
-        total = tok[t, :, QUART:].astype(F32) + mixed(way, 0, ret_b[way, yh])
+            e = x_at(4 - j)
+            arrive(ids[way, "rb", 0, j], ret_b.at[way, yh, e], x_dev(4 - j))
+            total = total + mixed(way, 0, e, ret_b[way, yh, e])
         arrive(ids[way, "uy"], mix_in.at[way], y_dev)
         fin[way, :, QUART:] = (total + mix_in[way].astype(F32)).astype(BF16)
+        total = tok[t, :, :QUART].astype(F32) + mixed(way, 0, x, ret_a[way, x])
         for j in (1, 3, 2):
-            arrive(ids[way, "ra", j], ret_a.at[way, x_at(4 - j)], x_dev(4 - j))
-        fin[way, :, :QUART] = (tok[t, :, :QUART].astype(F32) + mixed(way, 0, ret_a[way])).astype(BF16)
+            e = x_at(4 - j)
+            arrive(ids[way, "ra", j], ret_a.at[way, e], x_dev(4 - j))
+            total = total + mixed(way, 0, e, ret_a[way, e])
+        fin[way, :, :QUART] = total.astype(BF16)
         out = (nxt, gin)[way]
         ids[way, "out"] = send(fin.at[way, lines(oc), :], out.at[:, half(c)], core_dev)[0]
         ids[way, "mine"] = local(fin.at[way, lines(c), :], out.at[:, half(c)])
@@ -315,12 +321,12 @@
     stage1(FWD)
     for copy in weights:
         copy.wait()
+    stage2(COT)
     stage3(SAVED)
     stage4(SAVED)
     before(oy)
-    stage2(COT)
+    stage2(FWD)
     before(yh)
-    stage2(FWD)
     stage3(COT)
     stage4(COT)
     backward(oy)
@@ -390,7 +396,7 @@
         pltpu.VMEM((2, group_rows, 2 * HID), BF16),
         pltpu.SemaphoreType.DMA((N_COPY,)),
         pltpu.SemaphoreType.DMA((N_COPY,)),
-        pltpu.SemaphoreType.DMA((16,)),
+        pltpu.SemaphoreType.DMA((9,)),
     ]
     rows_all = 2 * group_rows
     vmem = pl.BlockSpec(memory_space=pltpu.VMEM)

time: 132 us -> 130 us (0.985)
  Pallas kernels: 131 us -> 129 us
where the time goes in v4:
time: 130 us
  Pallas kernels  129 us (99%)
    pallas_call x1, Pallas kernels, body(): pl.pallas_call(kernel, name='relay_tick', out_shape=tuple((pltpu.VMEM(sha...  126 us
    pallas_call x1, Pallas kernels, body(): pl.pallas_call(write_out, name='write_out', out_shape=tuple((jax.ShapeDty...  3.09 us

profile of v4, /device:TPU:1, one launch (start us, length us, event | category | flops | bytes accessed | tf_op | source)
XLA Modules:
  0.0 130.2 jit_solution(10906246669874629394)
XLA Ops:
  0.6 126.3 %relay_tick.1 = (bf16[128,2048]{1,0:T(8,128)(2,1)S(1)}, bf16[128,2048]{1,0:T(8,128)(2,1)S(1)}, f32[2048,256]{1,0:T(8,128)S(1)}, f32[2048,256]{1,0:T(8,128)S(1)}, f32[256,2048]{1,0:T(8,128)S(1)}) custom-call(bf16[128,2048]{1,0:T(8,128)(2,1)} %bitcast.29, bf16[128,2048]{1,0:T(8,128)(2,1)} %bitcast.30, bf16[128,2048]{1,0:T(8,128)(2,1)} %bitcast.31, ...), custom_call_target="tpu_custom_call" | custom-call | flops 13287555072 | bytes 12582912 | tf_op jit(solution)/shard_map/relay_tick/pallas_call | solution.py:404
  126.9 3.1 %write_out.1 = (bf16[128,2048]{1,0:T(8,128)(2,1)}, bf16[128,2048]{1,0:T(8,128)(2,1)}, f32[2048,256]{1,0:T(8,128)}, f32[2048,256]{1,0:T(8,128)}, f32[256,2048]{1,0:T(8,128)}) custom-call(bf16[128,2048]{1,0:T(8,128)(2,1)S(1)} %get-tuple-element.15.refs_0_, bf16[128,2048]{1,0:T(8,128)(2,1)S(1)} %get-tuple-element.16.refs_1_, ...), custom_call_target="tpu_custom_call" | custom-call | tf_op jit(solution)/shard_map/write_out/pallas_call | solution.py:414

commit v5 on v4

--- a/solution.py
+++ b/solution.py
@@ -14,6 +14,8 @@
 QUART = D // 4
 HID = 256
 SAVED, FWD, COT = 0, 1, 2
+A_WIDE = {SAVED: QUART, FWD: 384, COT: QUART}
+B_MOST = HALF - 384
 N_COPY = 79
 MESH = pl.DeviceIdType.MESH
 F32 = jnp.float32
@@ -76,8 +78,11 @@
         copy.start()
         return copy
 
-    def cols(core, quarter):
-        return pl.ds(pl.multiple_of(core * HALF + quarter * QUART, QUART), QUART)
+    def width(t, part_of):
+        return HALF - A_WIDE[t] if part_of else A_WIDE[t]
+
+    def cols(t, core, part_of):
+        return pl.ds(pl.multiple_of(core * HALF + part_of * A_WIDE[t], 128), width(t, part_of))
 
     def half(core):
         return pl.ds(pl.multiple_of(core * HALF, HALF), HALF)
@@ -99,8 +104,8 @@
     i_r3, _ = send(routes, rts.at[2 + c], diag_dev)
     i_saved, _ = send(saved.at[:, half(oc)], tok.at[SAVED, lines(c), :], core_dev)
     i_b1 = [
-        send(saved.at[:, cols(c, 1)], toky.at[SAVED, lines(c), :], y_dev)[0],
-        send(saved.at[:, cols(oc, 1)], toky.at[SAVED, lines(c), :], diag_dev)[0],
+        send(saved.at[:, cols(SAVED, c, 1)], toky.at[SAVED, lines(c), pl.ds(0, width(SAVED, 1))], y_dev)[0],
+        send(saved.at[:, cols(SAVED, oc, 1)], toky.at[SAVED, lines(c), pl.ds(0, width(SAVED, 1))], diag_dev)[0],
     ]
     i_back = [send(returned.at[:, half(lax.rem(c + dc, 2))], tok.at[COT, lines(c), :], sec_dev(-1, dc))[0] for dc in (0, 1)]
     i_carry = [send(carried.at[:, half(lax.rem(c + dc, 2))], tok.at[FWD, lines(c), :], sec_dev(1, dc))[0] for dc in (0, 1)]
@@ -136,53 +141,53 @@
 
     def stage1(t):
         if t != SAVED:
-            ids[t, "b1"] = send(tok.at[t, :, pl.ds(QUART, QUART)], toky.at[t], y_dev)[0]
+            ids[t, "b1"] = send(tok.at[t, :, pl.ds(width(t, 0), width(t, 1))], toky.at[t, :, pl.ds(0, width(t, 1))], y_dev)[0]
         for j in (2, 1, 3, 0):
-            block = picked(t, 0, x_at(j), tok[t, :, :QUART])
+            block = picked(t, 0, x_at(j), tok[t, :, : width(t, 0)])
             if j:
-                pack_a[t, j - 1] = block
-                ids[t, "xa", j] = send(pack_a.at[t, j - 1], rows.at[t, yh, x, :, cols(c, 0)], x_dev(j))[0]
+                pack_a[t, j - 1, :, : width(t, 0)] = block
+                ids[t, "xa", j] = send(pack_a.at[t, j - 1, :, pl.ds(0, width(t, 0))], rows.at[t, yh, x, :, cols(t, c, 0)], x_dev(j))[0]
             else:
-                rows[t, yh, x, :, cols(c, 0)] = block
+                rows[t, yh, x, :, cols(t, c, 0)] = block
 
     def stage2(t):
         if t == SAVED:
-            arrive(i_b1[0], toky.at[t, lines(c), :], y_dev)
-            arrive(i_b1[1], toky.at[t, lines(oc), :], diag_dev)
+            arrive(i_b1[0], toky.at[t, lines(c), pl.ds(0, width(t, 1))], y_dev)
+            arrive(i_b1[1], toky.at[t, lines(oc), pl.ds(0, width(t, 1))], diag_dev)
         else:
-            arrive(ids[t, "b1"], toky.at[t], y_dev)
+            arrive(ids[t, "b1"], toky.at[t, :, pl.ds(0, width(t, 1))], y_dev)
         for j in (2, 1, 3, 0):
             for where, hh in ((0, yh), (1, oy)):
-                tokens = tok[t, :, QUART:] if where == 0 else toky[t]
+                tokens = tok[t, :, width(t, 0) :] if where == 0 else toky[t, :, : width(t, 1)]
                 block = picked(t, where, x_at(j), tokens)
                 if j:
-                    pack_b[t, j - 1, hh] = block
+                    pack_b[t, j - 1, hh, :, : width(t, 1)] = block
                 else:
-                    rows[t, hh, x, :, cols(c, 1)] = block
+                    rows[t, hh, x, :, cols(t, c, 1)] = block
             if j:
-                ids[t, "xb", j] = send(pack_b.at[t, j - 1], rows.at[t, :, x, :, cols(c, 1)], x_dev(j))[0]
+                ids[t, "xb", j] = send(pack_b.at[t, j - 1, :, :, pl.ds(0, width(t, 1))], rows.at[t, :, x, :, cols(t, c, 1)], x_dev(j))[0]
         for j in (0, 1, 3, 2):
-            place = rows.at[t, yh, x_at(4 - j), :, cols(c, 0)]
+            place = rows.at[t, yh, x_at(4 - j), :, cols(t, c, 0)]
             if j:
                 arrive(ids[t, "xa", j], place, x_dev(4 - j))
             ids[t, "ya", j] = send(place, place, y_dev)
-        place = rows.at[t, yh, :, :, cols(c, 0)]
+        place = rows.at[t, yh, :, :, cols(t, c, 0)]
         ids[t, "c0"] = send(place, place, core_dev)
 
     def stage3(t):
         for j in (0, 1, 3, 2):
-            arrive(ids[t, "ya", j][0], rows.at[t, oy, x_at(4 - j), :, cols(c, 0)], y_dev)
-        place = rows.at[t, oy, :, :, cols(c, 0)]
+            arrive(ids[t, "ya", j][0], rows.at[t, oy, x_at(4 - j), :, cols(t, c, 0)], y_dev)
+        place = rows.at[t, oy, :, :, cols(t, c, 0)]
         ids[t, "c1"] = send(place, place, core_dev)
         for j in (1, 3, 2):
-            arrive(ids[t, "xb", j], rows.at[t, :, x_at(4 - j), :, cols(c, 1)], x_dev(4 - j))
-        place = rows.at[t, :, :, :, cols(c, 1)]
+            arrive(ids[t, "xb", j], rows.at[t, :, x_at(4 - j), :, cols(t, c, 1)], x_dev(4 - j))
+        place = rows.at[t, :, :, :, cols(t, c, 1)]
         ids[t, "c2"] = send(place, place, core_dev)
 
     def stage4(t):
-        arrive(ids[t, "c0"][0], rows.at[t, yh, :, :, cols(oc, 0)], core_dev)
-        arrive(ids[t, "c1"][0], rows.at[t, oy, :, :, cols(oc, 0)], core_dev)
-        arrive(ids[t, "c2"][0], rows.at[t, :, :, :, cols(oc, 1)], core_dev)
+        arrive(ids[t, "c0"][0], rows.at[t, yh, :, :, cols(t, oc, 0)], core_dev)
+        arrive(ids[t, "c1"][0], rows.at[t, oy, :, :, cols(t, oc, 0)], core_dev)
+        arrive(ids[t, "c2"][0], rows.at[t, :, :, :, cols(t, oc, 1)], core_dev)
 
     def group(t, hh):
         return rows[t, hh].reshape(E_WIN * SLOT, D)
@@ -370,9 +375,9 @@
     group_rows = E_WIN * SLOT
     scratch = [
         pltpu.VMEM((3, CHIP, HALF), BF16),
-        pltpu.VMEM((3, CHIP, QUART), BF16),
+        pltpu.VMEM((3, CHIP, B_MOST), BF16),
         pltpu.VMEM((3, 3, SLOT, QUART), BF16),
-        pltpu.VMEM((3, 3, 2, SLOT, QUART), BF16),
+        pltpu.VMEM((3, 3, 2, SLOT, B_MOST), BF16),
         pltpu.VMEM((3, 2, E_WIN, SLOT, D), BF16),
         pltpu.VMEM((D, HID), BF16),
         pltpu.VMEM((D, HID), BF16),

time: 130 us -> 132 us (1.015)
  Pallas kernels: 129 us -> 131 us
    pallas_call x1, Pallas kernels: 126 us -> 128 us  [body(): pl.pallas_call(kernel, name='relay_tick', out_shape=tuple((pltpu.VMEM(sha...]
where the time goes in v5:
time: 132 us
  Pallas kernels  131 us (99%)
    pallas_call x1, Pallas kernels, body(): pl.pallas_call(kernel, name='relay_tick', out_shape=tuple((pltpu.VMEM(sha...  128 us
    pallas_call x1, Pallas kernels, body(): pl.pallas_call(write_out, name='write_out', out_shape=tuple((jax.ShapeDty...  3.09 us

profile of v5, /device:TPU:1, one launch (start us, length us, event | category | flops | bytes accessed | tf_op | source)
XLA Modules:
  0.0 131.8 jit_solution(12921586863530362225)
XLA Ops:
  0.6 127.9 %relay_tick.1 = (bf16[128,2048]{1,0:T(8,128)(2,1)S(1)}, bf16[128,2048]{1,0:T(8,128)(2,1)S(1)}, f32[2048,256]{1,0:T(8,128)S(1)}, f32[2048,256]{1,0:T(8,128)S(1)}, f32[256,2048]{1,0:T(8,128)S(1)}) custom-call(bf16[128,2048]{1,0:T(8,128)(2,1)} %bitcast.29, bf16[128,2048]{1,0:T(8,128)(2,1)} %bitcast.30, bf16[128,2048]{1,0:T(8,128)(2,1)} %bitcast.31, ...), custom_call_target="tpu_custom_call" | custom-call | flops 13287555072 | bytes 12582912 | tf_op jit(solution)/shard_map/relay_tick/pallas_call | solution.py:409
  128.5 3.1 %write_out.1 = (bf16[128,2048]{1,0:T(8,128)(2,1)}, bf16[128,2048]{1,0:T(8,128)(2,1)}, f32[2048,256]{1,0:T(8,128)}, f32[2048,256]{1,0:T(8,128)}, f32[256,2048]{1,0:T(8,128)}) custom-call(bf16[128,2048]{1,0:T(8,128)(2,1)S(1)} %get-tuple-element.15.refs_0_, bf16[128,2048]{1,0:T(8,128)(2,1)S(1)} %get-tuple-element.16.refs_1_, ...), custom_call_target="tpu_custom_call" | custom-call | tf_op jit(solution)/shard_map/write_out/pallas_call | solution.py:419
